TPU v7x, 256 devices: a whole 4x4x8 slice. The times are simulated.
256 devices in a mesh: seq: 64 (over z, y, core), mp: 4 (over x).
Axes of the slice: x: 4, y: 4, z: 8, core: 2. Of those that a mesh axis runs over, the one named last changes fastest.
Arguments:
- se_query: bfloat16 [8192, 8192], P('seq', 'mp'), may hold values from -6 to 6
- se_key: bfloat16 [8192, 8192], P('seq', 'mp'), may hold values from -6 to 6
- se_value: bfloat16 [8192, 8192], P('seq', 'mp'), may hold values from -6 to 6
- mr_query: bfloat16 [8192, 8192], P('seq', 'mp'), may hold values from -6 to 6
- mr_key: bfloat16 [8192, 8192], P('seq', 'mp'), may hold values from -6 to 6
- att_query: bfloat16 [8192, 8192], P('seq', 'mp'), may hold values from -52 to 52
- att_key: bfloat16 [8192, 8192], P('seq', 'mp'), may hold values from -6 to 6
- doc_ids: int32 [8192], P('seq'), may hold values from 0 to 127, never falling along the last dimension, each value on 1 to 1024 neighbouring positions
- se_taps: float32 [7, 8192], P(None, 'mp'), may hold values from -2.4 to 2.4
- mr_taps: bfloat16 [128, 8192], P(None, 'mp'), may hold values from -1.796875 to 1.796875
- mr_rates: float32 [8192], P('mp'), may hold values from 0.003 to 0.1
- se_gain: float32 [8192], P('mp'), may hold values from 0.1 to 1.9
- mr_gain: float32 [8192], P('mp'), may hold values from 0.1 to 1.9
- att_gain: float32 [8192], P('mp'), may hold values from 0.1 to 1.9
Outputs:
- mr_out: bfloat16 [8192, 8192], P('seq', 'mp')
- att_out: bfloat16 [8192, 8192], P('seq', 'mp')
Inputs may be any that keep to these rules, and one draw needn't show every extreme that they name: `doc_ids`: document ids never fall along the pack; each document has 1 to 1024 tokens and one has exactly 1024.
All inputs are finite; a program needn't handle non-finite values.
Results may differ from a plain program's by a relative error of at most 0.017.
Values may be sent and summed in bfloat16 or wider, within the bound.
A program may use at most 64 MiB of HBM per device.

v0:
```python
import jax
import jax.numpy as jnp
from jax import lax
from jax.sharding import PartitionSpec as P

D = 8192
HEAD_DIM = 128


def shifted(value, axis, steps):
    count = lax.axis_size(axis)
    first, last = (max(0, -steps), min(count, count - steps))
    return lax.ppermute(value, axis, [(source, source + steps) for source in range(first, last)])


def causal_filter(local_u, prior_u, local_ids, prior_ids, taps):
    tap_count = taps.shape[0]
    row_count, channels = local_u.shape
    extended = jnp.concatenate([prior_u, local_u], 0)
    ext_ids = jnp.concatenate([prior_ids[prior_ids.shape[0] - (tap_count - 1) :], local_ids], 0)
    tap_group = 16 if tap_count % 16 == 0 else tap_count

    def add_group(outer_step, running):
        for offset in range(tap_group):
            tap_index = outer_step * tap_group + offset
            start = (tap_count - 1 - tap_index).astype(jnp.int32)
            window_rows = lax.dynamic_slice_in_dim(extended, start, row_count, 0).astype(
                jnp.float32
            )
            window_ids = lax.dynamic_slice_in_dim(ext_ids, start, row_count, 0)
            tap_row = lax.dynamic_index_in_dim(taps, tap_index, 0, keepdims=False)
            running = running + jnp.where(
                (window_ids == local_ids)[:, None], window_rows * tap_row[None, :], 0.0
            )
        return running

    return lax.fori_loop(
        0, tap_count // tap_group, add_group, jnp.zeros((row_count, channels), jnp.float32)
    )


def width_norm(layer_out, gain):
    total = lax.psum(jnp.sum(layer_out * layer_out, axis=1), "mp")
    return (layer_out * lax.rsqrt(total / D + 1e-06)[:, None] * gain[None, :]).astype(jnp.bfloat16)


def local(
    se_query,
    se_key,
    se_value,
    mr_query,
    mr_key,
    att_query,
    att_key,
    doc_ids,
    se_taps,
    mr_taps,
    mr_rates,
    se_gain,
    mr_gain,
    att_gain,
):
    row_count, channels = se_query.shape
    mr_span = mr_taps.shape[0] - 1
    se_span = se_taps.shape[0] - 1
    se_u = (se_key.astype(jnp.float32) * se_value.astype(jnp.float32)).astype(jnp.bfloat16)
    prior_se, prior_ids = shifted(
        (se_u[row_count - se_span :], doc_ids[row_count - mr_span :]), "seq", 1
    )
    se_y = se_query.astype(jnp.float32) * causal_filter(se_u, prior_se, doc_ids, prior_ids, se_taps)
    se_out = width_norm(se_y, se_gain)
    mr_u = (mr_key.astype(jnp.float32) * se_out.astype(jnp.float32)).astype(jnp.bfloat16)
    prior_mr = shifted(mr_u[row_count - mr_span :], "seq", 1)
    tap_pos = jnp.arange(mr_taps.shape[0]).astype(jnp.float32)[:, None]
    mr_filter = mr_taps.astype(jnp.float32) * jnp.exp(-mr_rates[None, :] * tap_pos)
    mr_y = mr_query.astype(jnp.float32) * causal_filter(
        mr_u, prior_mr, doc_ids, prior_ids, mr_filter
    )
    mr_out = width_norm(mr_y, mr_gain)
    head_count = channels // HEAD_DIM
    queries = att_query.reshape(row_count, head_count, HEAD_DIM)
    score_scale = HEAD_DIM ** (-0.5)
    reach = max(1, min(8, lax.axis_size("seq") // 8))
    my_index = lax.axis_index("seq")

    def block_scores(key_rows, key_ids, extra):
        scores = (
            jnp.einsum(
                "qhd,khd->hqk",
                queries,
                key_rows.reshape(row_count, head_count, HEAD_DIM),
                preferred_element_type=jnp.float32,
            )
            * score_scale
        )
        allowed = (doc_ids[:, None] == key_ids[None, :]) & extra
        return (jnp.where(allowed[None], scores, -1e30), allowed)

    causal = jnp.arange(row_count)[:, None] >= jnp.arange(row_count)[None, :]
    local_scores, local_allowed = block_scores(att_key, doc_ids, causal)
    blocks = [(mr_out, local_scores, local_allowed)]
    carried = (att_key, mr_out, doc_ids)
    for distance in range(1, reach + 1):
        carried = shifted((carried[0], carried[1], carried[2]), "seq", 1)
        got_scores, got_allowed = block_scores(carried[0], carried[2], my_index >= distance)
        blocks.append((carried[1], got_scores, got_allowed))
    row_max = blocks[0][1].max(axis=2, keepdims=True)
    for entry in blocks[1:]:
        row_max = jnp.maximum(row_max, entry[1].max(axis=2, keepdims=True))
    denom = jnp.zeros_like(row_max)
    for entry in blocks:
        denom = denom + jnp.sum(
            jnp.where(entry[2][None], jnp.exp(entry[1] - row_max), 0.0), axis=2, keepdims=True
        )
    mixed = jnp.zeros((row_count, head_count, HEAD_DIM), jnp.float32)
    for entry in blocks:
        weights = (jnp.where(entry[2][None], jnp.exp(entry[1] - row_max), 0.0) / denom).astype(
            jnp.bfloat16
        )
        mixed = mixed + jnp.einsum(
            "hqk,khd->qhd",
            weights,
            entry[0].reshape(row_count, head_count, HEAD_DIM),
            preferred_element_type=jnp.float32,
        )
    att_y = mixed.reshape(row_count, channels)
    return (mr_out, width_norm(att_y, att_gain))


def solution(mesh):
    return jax.shard_map(
        local,
        mesh=mesh,
        in_specs=(
            P("seq", "mp"),
            P("seq", "mp"),
            P("seq", "mp"),
            P("seq", "mp"),
            P("seq", "mp"),
            P("seq", "mp"),
            P("seq", "mp"),
            P("seq"),
            P(None, "mp"),
            P(None, "mp"),
            P("mp"),
            P("mp"),
            P("mp"),
            P("mp"),
        ),
        out_specs=(P("seq", "mp"), P("seq", "mp")),
        check_vma=False,
    )
```

profile of v0, /device:TPU:128, one launch (start us, length us, event | category | flops | bytes accessed | tf_op | source)
XLA Modules:
  0.0 305.3 jit_solution(11810980229393243340)
XLA Ops:
  15.9 10.5 %psum.21 = f32[128]{0:T(128)S(1)} all-reduce(f32[128]{0:T(128)S(1)} %get-tuple-element.297), channel_id=1, replica_groups=mesh['seq'=64,'mp'=4] {'mp'}, use_global_device_ids=true, to_apply=%region_1.2 | all-reduce | flops 128 | bytes 1024 | tf_op jit(solution)/shard_map/psum | solution.py:43
  33.0 8.7 %collective-permute-done.2 = bf16[127,2048]{1,0:T(8,128)(2,1)S(1)} collective-permute-done((bf16[127,2048]{1,0:T(8,128)(2,1)S(1)}, bf16[127,2048]{1,0:T(8,128)(2,1)S(1)}, u32[]{:S(2)}, u32[]{:S(2)}) %collective-permute-start.2) | collective-permute-done | bytes 520224 | tf_op jit(solution)/shard_map/ppermute | solution.py:13
  41.9 60.5 %while.22 = (s32[]{:T(128)}, f32[128,2048]{1,0:T(8,128)S(1)}, s32[255]{0:T(256)S(1)}, s32[128]{0:T(128)S(1)}, bf16[255,2048]{1,0:T(8,128)(2,1)S(1)}, /*index=5*/...) while((s32[]{:T(128)}, f32[128,2048]{1,0:T(8,128)S(1)}, ...), condition=%wide.region_3.4_spmd.clone, body=%wide.region_2.3_spmd.clone.sunk | while | flops 17041540 | bytes 10893807 | solution.py:37
  44.2 5.3 %fusion.141 = f32[128,2048]{1,0:T(8,128)S(1)} fusion(f32[128,2048]{1,0:T(8,128)S(1)} %get-tuple-element.516, f32[2048]{0:T(1024)S(1)} %bitcast.171, bf16[255,2048]{1,0:T(8,128)(2,1)S(1)} %get-tuple-element.560, s32[]{:T(128)S(6)} %select_n.917, f32[2048]{0:T(1024)S(1)} %bitcast.172, s32[]{:T(128)S(6)} %select_n.918, f32[2048]{0:T(1024)S(1)} %bitcast.173, ...), kind=kLoop, calls=%fused_computation.15.clone.1 | loop fusion | flops 17039360 | bytes 10618945 | tf_op jit(solution)/shard_map/while/body/eval_jaxpr/add | solution.py:32
  51.8 5.3 %fusion.141 = f32[128,2048]{1,0:T(8,128)S(1)} fusion(f32[128,2048]{1,0:T(8,128)S(1)} %get-tuple-element.516, f32[2048]{0:T(1024)S(1)} %bitcast.171, bf16[255,2048]{1,0:T(8,128)(2,1)S(1)} %get-tuple-element.560, s32[]{:T(128)S(6)} %select_n.917, f32[2048]{0:T(1024)S(1)} %bitcast.172, s32[]{:T(128)S(6)} %select_n.918, f32[2048]{0:T(1024)S(1)} %bitcast.173, ...), kind=kLoop, calls=%fused_computation.15.clone.1 | loop fusion | flops 17039360 | bytes 10618945 | tf_op jit(solution)/shard_map/while/body/eval_jaxpr/add | solution.py:32
  59.2 5.3 %fusion.141 = f32[128,2048]{1,0:T(8,128)S(1)} fusion(f32[128,2048]{1,0:T(8,128)S(1)} %get-tuple-element.516, f32[2048]{0:T(1024)S(1)} %bitcast.171, bf16[255,2048]{1,0:T(8,128)(2,1)S(1)} %get-tuple-element.560, s32[]{:T(128)S(6)} %select_n.917, f32[2048]{0:T(1024)S(1)} %bitcast.172, s32[]{:T(128)S(6)} %select_n.918, f32[2048]{0:T(1024)S(1)} %bitcast.173, ...), kind=kLoop, calls=%fused_computation.15.clone.1 | loop fusion | flops 17039360 | bytes 10618945 | tf_op jit(solution)/shard_map/while/body/eval_jaxpr/add | solution.py:32
  66.8 5.3 %fusion.141 = f32[128,2048]{1,0:T(8,128)S(1)} fusion(f32[128,2048]{1,0:T(8,128)S(1)} %get-tuple-element.516, f32[2048]{0:T(1024)S(1)} %bitcast.171, bf16[255,2048]{1,0:T(8,128)(2,1)S(1)} %get-tuple-element.560, s32[]{:T(128)S(6)} %select_n.917, f32[2048]{0:T(1024)S(1)} %bitcast.172, s32[]{:T(128)S(6)} %select_n.918, f32[2048]{0:T(1024)S(1)} %bitcast.173, ...), kind=kLoop, calls=%fused_computation.15.clone.1 | loop fusion | flops 17039360 | bytes 10618945 | tf_op jit(solution)/shard_map/while/body/eval_jaxpr/add | solution.py:32
  74.4 5.3 %fusion.141 = f32[128,2048]{1,0:T(8,128)S(1)} fusion(f32[128,2048]{1,0:T(8,128)S(1)} %get-tuple-element.516, f32[2048]{0:T(1024)S(1)} %bitcast.171, bf16[255,2048]{1,0:T(8,128)(2,1)S(1)} %get-tuple-element.560, s32[]{:T(128)S(6)} %select_n.917, f32[2048]{0:T(1024)S(1)} %bitcast.172, s32[]{:T(128)S(6)} %select_n.918, f32[2048]{0:T(1024)S(1)} %bitcast.173, ...), kind=kLoop, calls=%fused_computation.15.clone.1 | loop fusion | flops 17039360 | bytes 10618945 | tf_op jit(solution)/shard_map/while/body/eval_jaxpr/add | solution.py:32
  82.0 5.3 %fusion.141 = f32[128,2048]{1,0:T(8,128)S(1)} fusion(f32[128,2048]{1,0:T(8,128)S(1)} %get-tuple-element.516, f32[2048]{0:T(1024)S(1)} %bitcast.171, bf16[255,2048]{1,0:T(8,128)(2,1)S(1)} %get-tuple-element.560, s32[]{:T(128)S(6)} %select_n.917, f32[2048]{0:T(1024)S(1)} %bitcast.172, s32[]{:T(128)S(6)} %select_n.918, f32[2048]{0:T(1024)S(1)} %bitcast.173, ...), kind=kLoop, calls=%fused_computation.15.clone.1 | loop fusion | flops 17039360 | bytes 10618945 | tf_op jit(solution)/shard_map/while/body/eval_jaxpr/add | solution.py:32
  89.5 5.3 %fusion.141 = f32[128,2048]{1,0:T(8,128)S(1)} fusion(f32[128,2048]{1,0:T(8,128)S(1)} %get-tuple-element.516, f32[2048]{0:T(1024)S(1)} %bitcast.171, bf16[255,2048]{1,0:T(8,128)(2,1)S(1)} %get-tuple-element.560, s32[]{:T(128)S(6)} %select_n.917, f32[2048]{0:T(1024)S(1)} %bitcast.172, s32[]{:T(128)S(6)} %select_n.918, f32[2048]{0:T(1024)S(1)} %bitcast.173, ...), kind=kLoop, calls=%fused_computation.15.clone.1 | loop fusion | flops 17039360 | bytes 10618945 | tf_op jit(solution)/shard_map/while/body/eval_jaxpr/add | solution.py:32
  97.1 5.3 %fusion.141 = f32[128,2048]{1,0:T(8,128)S(1)} fusion(f32[128,2048]{1,0:T(8,128)S(1)} %get-tuple-element.516, f32[2048]{0:T(1024)S(1)} %bitcast.171, bf16[255,2048]{1,0:T(8,128)(2,1)S(1)} %get-tuple-element.560, s32[]{:T(128)S(6)} %select_n.917, f32[2048]{0:T(1024)S(1)} %bitcast.172, s32[]{:T(128)S(6)} %select_n.918, f32[2048]{0:T(1024)S(1)} %bitcast.173, ...), kind=kLoop, calls=%fused_computation.15.clone.1 | loop fusion | flops 17039360 | bytes 10618945 | tf_op jit(solution)/shard_map/while/body/eval_jaxpr/add | solution.py:32
  102.6 7.7 %psum.22 = f32[128]{0:T(128)S(1)} all-reduce(f32[128]{0:T(128)S(1)} %multiply_reduce_fusion), channel_id=1, replica_groups=mesh['seq'=64,'mp'=4] {'mp'}, use_global_device_ids=true, to_apply=%region_5.6 | all-reduce | flops 128 | bytes 1024 | tf_op jit(solution)/shard_map/psum | solution.py:43
  114.4 10.0 %collective-permute-done.19 = bf16[128,2048]{1,0:T(8,128)(2,1)S(1)} collective-permute-done((bf16[128,2048]{1,0:T(8,128)(2,1)S(1)}, bf16[128,2048]{1,0:T(8,128)(2,1)S(1)}, u32[]{:S(2)}, u32[]{:S(2)}) %collective-permute-start.19) | collective-permute-done | bytes 524320 | tf_op jit(solution)/shard_map/ppermute | solution.py:13
  133.9 10.1 %collective-permute-done.3 = s32[128]{0:T(128)S(1)} collective-permute-done((s32[128]{0:T(128)S(1)}, s32[128]{0:T(128)S(1)}, u32[]{:S(2)}, u32[]{:S(2)}) %collective-permute-start.3) | collective-permute-done | bytes 544 | tf_op jit(solution)/shard_map/ppermute | solution.py:13
  145.8 6.3 %collective-permute-done.5 = s32[128]{0:T(128)S(1)} collective-permute-done((s32[128]{0:T(128)S(1)}, s32[128]{0:T(128)S(1)}, u32[]{:S(2)}, u32[]{:S(2)}) %collective-permute-start.5) | collective-permute-done | bytes 544 | tf_op jit(solution)/shard_map/ppermute | solution.py:13
  154.0 6.3 %collective-permute-done.7 = s32[128]{0:T(128)S(1)} collective-permute-done((s32[128]{0:T(128)S(1)}, s32[128]{0:T(128)S(1)}, u32[]{:S(2)}, u32[]{:S(2)}) %collective-permute-start.7) | collective-permute-done | bytes 544 | tf_op jit(solution)/shard_map/ppermute | solution.py:13
  162.2 6.3 %collective-permute-done.9 = s32[128]{0:T(128)S(1)} collective-permute-done((s32[128]{0:T(128)S(1)}, s32[128]{0:T(128)S(1)}, u32[]{:S(2)}, u32[]{:S(2)}) %collective-permute-start.9) | collective-permute-done | bytes 544 | tf_op jit(solution)/shard_map/ppermute | solution.py:13
  170.3 6.3 %collective-permute-done.11 = s32[128]{0:T(128)S(1)} collective-permute-done((s32[128]{0:T(128)S(1)}, s32[128]{0:T(128)S(1)}, u32[]{:S(2)}, u32[]{:S(2)}) %collective-permute-start.11) | collective-permute-done | bytes 544 | tf_op jit(solution)/shard_map/ppermute | solution.py:13
  178.5 6.3 %collective-permute-done.13 = s32[128]{0:T(128)S(1)} collective-permute-done((s32[128]{0:T(128)S(1)}, s32[128]{0:T(128)S(1)}, u32[]{:S(2)}, u32[]{:S(2)}) %collective-permute-start.13) | collective-permute-done | bytes 544 | tf_op jit(solution)/shard_map/ppermute | solution.py:13
  186.7 6.2 %collective-permute-done.15 = s32[128]{0:T(128)S(1)} collective-permute-done((s32[128]{0:T(128)S(1)}, s32[128]{0:T(128)S(1)}, u32[]{:S(2)}, u32[]{:S(2)}) %collective-permute-start.15) | collective-permute-done | bytes 544 | tf_op jit(solution)/shard_map/ppermute | solution.py:13
  194.9 6.2 %collective-permute-done.17 = s32[128]{0:T(128)S(1)} collective-permute-done((s32[128]{0:T(128)S(1)}, s32[128]{0:T(128)S(1)}, u32[]{:S(2)}, u32[]{:S(2)}) %collective-permute-start.17) | collective-permute-done | bytes 544 | tf_op jit(solution)/shard_map/ppermute | solution.py:13
  209.3 6.2 %collective-permute-done.21 = bf16[128,2048]{1,0:T(8,128)(2,1)} collective-permute-done((bf16[128,2048]{1,0:T(8,128)(2,1)}, bf16[128,2048]{1,0:T(8,128)(2,1)}, u32[]{:S(2)}, u32[]{:S(2)}) %collective-permute-start.21) | collective-permute-done | bytes 524320 | tf_op jit(solution)/shard_map/ppermute | solution.py:13
  285.7 6.6 %collective-permute-done.26 = bf16[128,2048]{1,0:T(8,128)(2,1)S(1)} collective-permute-done((bf16[128,2048]{1,0:T(8,128)(2,1)}, bf16[128,2048]{1,0:T(8,128)(2,1)S(1)}, u32[]{:S(2)}, u32[]{:S(2)}) %collective-permute-start.26) | collective-permute-done | bytes 524320 | tf_op jit(solution)/shard_map/ppermute | solution.py:13
  294.6 9.8 %psum.23 = f32[128]{0:T(128)S(1)} all-reduce(f32[128]{0:T(128)S(1)} %get-tuple-element.371), channel_id=1, replica_groups=mesh['seq'=64,'mp'=4] {'mp'}, use_global_device_ids=true, to_apply=%region_25.26 | all-reduce | flops 128 | bytes 1024 | tf_op jit(solution)/shard_map/psum | solution.py:43
  (167 shorter events, 146.5 us)
Async XLA Ops:
  1.5 10.0 %collective-permute-start = (s32[127]{0:T(128)S(1)}, s32[127]{0:T(128)S(1)}, u32[]{:S(2)}, u32[]{:S(2)}) collective-permute-start(s32[127]{0:T(128)S(1)} %slice.33), channel_id=1, source_target_pairs={{0,4},{4,8},{8,12},{12,16},{16,20},{20,24},{24,28},{28,32},{32,36}... | collective-permute-start | bytes 1532 | tf_op jit(solution)/shard_map/ppermute | solution.py:13
  4.9 8.6 %collective-permute-start.1 = (bf16[6,2048]{1,0:T(8,128)(2,1)S(1)}, bf16[6,2048]{1,0:T(8,128)(2,1)S(1)}, u32[]{:S(2)}, u32[]{:S(2)}) collective-permute-start(bf16[6,2048]{1,0:T(8,128)(2,1)S(1)} %slice.37), channel_id=1, source_target_pairs={{0,4},{4,8},{8,12},{12,16},{16,20},{20,24},{24,28},{28,32},{32,36}... | collective-permute-start | bytes 73736 | tf_op jit(solution)/shard_map/ppermute | solution.py:13
  9.5 21.6 %collective-permute-start.4 = (bf16[128,2048]{0,1:T(8,128)(2,1)}, bf16[128,2048]{0,1:T(8,128)(2,1)}, u32[]{:S(2)}, u32[]{:S(2)}) collective-permute-start(bf16[128,2048]{0,1:T(8,128)(2,1)} %copy.47), channel_id=1, source_target_pairs={{0,4},{4,8},{8,12},{12,16},{16,20},{20,24},{24,28},{28,32},{32,36}... | collective-permute-start | bytes 1572872 | tf_op jit(solution)/shard_map/ppermute | solution.py:13
  27.9 13.8 %collective-permute-start.2 = (bf16[127,2048]{1,0:T(8,128)(2,1)S(1)}, bf16[127,2048]{1,0:T(8,128)(2,1)S(1)}, u32[]{:S(2)}, u32[]{:S(2)}) collective-permute-start(bf16[127,2048]{1,0:T(8,128)(2,1)S(1)} %slice.38), channel_id=1, source_target_pairs={{0,4},{4,8},{8,12},{12,16},{16,20},{20,24},{24,28},{28,32},{32,36}... | collective-permute-start | bytes 1560584 | tf_op jit(solution)/shard_map/ppermute | solution.py:13
  31.1 81.4 %collective-permute-start.6 = (bf16[128,2048]{0,1:T(8,128)(2,1)}, bf16[128,2048]{0,1:T(8,128)(2,1)}, u32[]{:S(2)}, u32[]{:S(2)}) collective-permute-start(bf16[128,2048]{0,1:T(8,128)(2,1)} %collective-permute-done.4), channel_id=1, source_target_pairs={{0,4},{4,8},{8,12},{12,16},{16,20},{20,24},{24,28},{28,32},{32,36}... | collective-permute-start | bytes 1572872 | tf_op jit(solution)/shard_map/ppermute | solution.py:13
  110.6 13.8 %collective-permute-start.19 = (bf16[128,2048]{1,0:T(8,128)(2,1)S(1)}, bf16[128,2048]{1,0:T(8,128)(2,1)S(1)}, u32[]{:S(2)}, u32[]{:S(2)}) collective-permute-start(bf16[128,2048]{1,0:T(8,128)(2,1)S(1)} %multiply_convert_fusion.1), channel_id=1, source_target_pairs={{0,4},{4,8},{8,12},{12,16},{16,20},{20,24},{24,28},{28,32},{32,36}... | collective-permute-start | bytes 1572872 | tf_op jit(solution)/shard_map/ppermute | solution.py:13
  112.5 17.5 %collective-permute-start.8 = (bf16[128,2048]{0,1:T(8,128)(2,1)}, bf16[128,2048]{0,1:T(8,128)(2,1)S(1)}, u32[]{:S(2)}, u32[]{:S(2)}) collective-permute-start(bf16[128,2048]{0,1:T(8,128)(2,1)} %collective-permute-done.6), channel_id=1, source_target_pairs={{0,4},{4,8},{8,12},{12,16},{16,20},{20,24},{24,28},{28,32},{32,36}... | collective-permute-start | bytes 1572872 | tf_op jit(solution)/shard_map/ppermute | solution.py:13
  124.4 76.9 %collective-permute-start.20 = (bf16[128,2048]{1,0:T(8,128)(2,1)S(1)}, bf16[128,2048]{1,0:T(8,128)(2,1)}, u32[]{:S(2)}, u32[]{:S(2)}) collective-permute-start(bf16[128,2048]{1,0:T(8,128)(2,1)S(1)} %collective-permute-done.19), channel_id=1, source_target_pairs={{0,4},{4,8},{8,12},{12,16},{16,20},{20,24},{24,28},{28,32},{32,36}... | collective-permute-start | bytes 1572872 | tf_op jit(solution)/shard_map/ppermute | solution.py:13
  130.0 73.3 %collective-permute-start.10 = (bf16[128,2048]{0,1:T(8,128)(2,1)S(1)}, bf16[128,2048]{0,1:T(8,128)(2,1)}, u32[]{:S(2)}, u32[]{:S(2)}) collective-permute-start(bf16[128,2048]{0,1:T(8,128)(2,1)S(1)} %collective-permute-done.8), channel_id=1, source_target_pairs={{0,4},{4,8},{8,12},{12,16},{16,20},{20,24},{24,28},{28,32},{32,36}... | collective-permute-start | bytes 1572872 | tf_op jit(solution)/shard_map/ppermute | solution.py:13
  131.9 12.0 %collective-permute-start.3 = (s32[128]{0:T(128)S(1)}, s32[128]{0:T(128)S(1)}, u32[]{:S(2)}, u32[]{:S(2)}) collective-permute-start(s32[128]{0:T(128)S(1)} %get-tuple-element.605), channel_id=1, source_target_pairs={{0,4},{4,8},{8,12},{12,16},{16,20},{20,24},{24,28},{28,32},{32,36}... | collective-permute-start | bytes 1544 | tf_op jit(solution)/shard_map/ppermute | solution.py:13
  143.9 8.2 %collective-permute-start.5 = (s32[128]{0:T(128)S(1)}, s32[128]{0:T(128)S(1)}, u32[]{:S(2)}, u32[]{:S(2)}) collective-permute-start(s32[128]{0:T(128)S(1)} %collective-permute-done.3), channel_id=1, source_target_pairs={{0,4},{4,8},{8,12},{12,16},{16,20},{20,24},{24,28},{28,32},{32,36}... | collective-permute-start | bytes 1544 | tf_op jit(solution)/shard_map/ppermute | solution.py:13
  152.1 8.2 %collective-permute-start.7 = (s32[128]{0:T(128)S(1)}, s32[128]{0:T(128)S(1)}, u32[]{:S(2)}, u32[]{:S(2)}) collective-permute-start(s32[128]{0:T(128)S(1)} %collective-permute-done.5), channel_id=1, source_target_pairs={{0,4},{4,8},{8,12},{12,16},{16,20},{20,24},{24,28},{28,32},{32,36}... | collective-permute-start | bytes 1544 | tf_op jit(solution)/shard_map/ppermute | solution.py:13
  160.3 8.2 %collective-permute-start.9 = (s32[128]{0:T(128)S(1)}, s32[128]{0:T(128)S(1)}, u32[]{:S(2)}, u32[]{:S(2)}) collective-permute-start(s32[128]{0:T(128)S(1)} %collective-permute-done.7), channel_id=1, source_target_pairs={{0,4},{4,8},{8,12},{12,16},{16,20},{20,24},{24,28},{28,32},{32,36}... | collective-permute-start | bytes 1544 | tf_op jit(solution)/shard_map/ppermute | solution.py:13
  192.9 8.2 %collective-permute-start.17 = (s32[128]{0:T(128)S(1)}, s32[128]{0:T(128)S(1)}, u32[]{:S(2)}, u32[]{:S(2)}) collective-permute-start(s32[128]{0:T(128)S(1)} %collective-permute-done.15), channel_id=1, source_target_pairs={{0,4},{4,8},{8,12},{12,16},{16,20},{20,24},{24,28},{28,32},{32,36}... | collective-permute-start | bytes 1544 | tf_op jit(solution)/shard_map/ppermute | solution.py:13
  201.3 14.1 %collective-permute-start.21 = (bf16[128,2048]{1,0:T(8,128)(2,1)}, bf16[128,2048]{1,0:T(8,128)(2,1)}, u32[]{:S(2)}, u32[]{:S(2)}) collective-permute-start(bf16[128,2048]{1,0:T(8,128)(2,1)} %collective-permute-done.20), channel_id=1, source_target_pairs={{0,4},{4,8},{8,12},{12,16},{16,20},{20,24},{24,28},{28,32},{32,36}... | collective-permute-start | bytes 1572872 | tf_op jit(solution)/shard_map/ppermute | solution.py:13
  203.3 17.8 %collective-permute-start.12 = (bf16[128,2048]{0,1:T(8,128)(2,1)}, bf16[128,2048]{0,1:T(8,128)(2,1)}, u32[]{:S(2)}, u32[]{:S(2)}) collective-permute-start(bf16[128,2048]{0,1:T(8,128)(2,1)} %collective-permute-done.10), channel_id=1, source_target_pairs={{0,4},{4,8},{8,12},{12,16},{16,20},{20,24},{24,28},{28,32},{32,36}... | collective-permute-start | bytes 1572872 | tf_op jit(solution)/shard_map/ppermute | solution.py:13
  215.5 14.1 %collective-permute-start.22 = (bf16[128,2048]{1,0:T(8,128)(2,1)}, bf16[128,2048]{1,0:T(8,128)(2,1)}, u32[]{:S(2)}, u32[]{:S(2)}) collective-permute-start(bf16[128,2048]{1,0:T(8,128)(2,1)} %collective-permute-done.21), channel_id=1, source_target_pairs={{0,4},{4,8},{8,12},{12,16},{16,20},{20,24},{24,28},{28,32},{32,36}... | collective-permute-start | bytes 1572872 | tf_op jit(solution)/shard_map/ppermute | solution.py:13
  221.1 14.1 %collective-permute-start.14 = (bf16[128,2048]{0,1:T(8,128)(2,1)}, bf16[128,2048]{0,1:T(8,128)(2,1)}, u32[]{:S(2)}, u32[]{:S(2)}) collective-permute-start(bf16[128,2048]{0,1:T(8,128)(2,1)} %collective-permute-done.12), channel_id=1, source_target_pairs={{0,4},{4,8},{8,12},{12,16},{16,20},{20,24},{24,28},{28,32},{32,36}... | collective-permute-start | bytes 1572872 | tf_op jit(solution)/shard_map/ppermute | solution.py:13
  229.6 17.0 %collective-permute-start.23 = (bf16[128,2048]{1,0:T(8,128)(2,1)}, bf16[128,2048]{1,0:T(8,128)(2,1)}, u32[]{:S(2)}, u32[]{:S(2)}) collective-permute-start(bf16[128,2048]{1,0:T(8,128)(2,1)} %collective-permute-done.22), channel_id=1, source_target_pairs={{0,4},{4,8},{8,12},{12,16},{16,20},{20,24},{24,28},{28,32},{32,36}... | collective-permute-start | bytes 1572872 | tf_op jit(solution)/shard_map/ppermute | solution.py:13
  235.2 14.1 %collective-permute-start.16 = (bf16[128,2048]{0,1:T(8,128)(2,1)}, bf16[128,2048]{0,1:T(8,128)(2,1)}, u32[]{:S(2)}, u32[]{:S(2)}) collective-permute-start(bf16[128,2048]{0,1:T(8,128)(2,1)} %collective-permute-done.14), channel_id=1, source_target_pairs={{0,4},{4,8},{8,12},{12,16},{16,20},{20,24},{24,28},{28,32},{32,36}... | collective-permute-start | bytes 1572872 | tf_op jit(solution)/shard_map/ppermute | solution.py:13
  246.6 14.1 %collective-permute-start.24 = (bf16[128,2048]{1,0:T(8,128)(2,1)}, bf16[128,2048]{1,0:T(8,128)(2,1)}, u32[]{:S(2)}, u32[]{:S(2)}) collective-permute-start(bf16[128,2048]{1,0:T(8,128)(2,1)} %collective-permute-done.23), channel_id=1, source_target_pairs={{0,4},{4,8},{8,12},{12,16},{16,20},{20,24},{24,28},{28,32},{32,36}... | collective-permute-start | bytes 1572872 | tf_op jit(solution)/shard_map/ppermute | solution.py:13
  249.3 17.0 %collective-permute-start.18 = (bf16[128,2048]{0,1:T(8,128)(2,1)}, bf16[128,2048]{0,1:T(8,128)(2,1)}, u32[]{:S(2)}, u32[]{:S(2)}) collective-permute-start(bf16[128,2048]{0,1:T(8,128)(2,1)} %collective-permute-done.16), channel_id=1, source_target_pairs={{0,4},{4,8},{8,12},{12,16},{16,20},{20,24},{24,28},{28,32},{32,36}... | collective-permute-start | bytes 1572872 | tf_op jit(solution)/shard_map/ppermute | solution.py:13
  262.8 15.3 %collective-permute-start.25 = (bf16[128,2048]{1,0:T(8,128)(2,1)}, bf16[128,2048]{1,0:T(8,128)(2,1)}, u32[]{:S(2)}, u32[]{:S(2)}) collective-permute-start(bf16[128,2048]{1,0:T(8,128)(2,1)} %collective-permute-done.24), channel_id=1, source_target_pairs={{0,4},{4,8},{8,12},{12,16},{16,20},{20,24},{24,28},{28,32},{32,36}... | collective-permute-start | bytes 1572872 | tf_op jit(solution)/shard_map/ppermute | solution.py:13
  278.1 14.2 %collective-permute-start.26 = (bf16[128,2048]{1,0:T(8,128)(2,1)}, bf16[128,2048]{1,0:T(8,128)(2,1)S(1)}, u32[]{:S(2)}, u32[]{:S(2)}) collective-permute-start(bf16[128,2048]{1,0:T(8,128)(2,1)} %collective-permute-done.25), channel_id=1, source_target_pairs={{0,4},{4,8},{8,12},{12,16},{16,20},{20,24},{24,28},{28,32},{32,36}... | collective-permute-start | bytes 1572872 | tf_op jit(solution)/shard_map/ppermute | solution.py:13
  (30 other events, 666.4 us)
where the time goes:
time: 308 us; the launch traced here: 305 us
  waiting for transfers between devices  103 us (33%)
  other arithmetic  56.2 us (18%)
  starting transfers between devices  53.8 us (17%)
  local copies, waits for them, and re-layouts  33.6 us (11%)
  blocking collectives  28 us (9%)
  matrix products  27.3 us (9%)
    ppermute x27, waiting for transfers between devices, shifted(): lax.ppermute(value, axis, [(source, source + steps) for source in range(f...  103 us
    ppermute x27, starting transfers between devices, shifted(): lax.ppermute(value, axis, [(source, source + steps) for source in range(f...  53.8 us
    add x8, other arithmetic, add_group(): running + jnp.where((window_ids == local_ids)[:, None], window_rows * tap...  42.1 us
    psum x3, blocking collectives, width_norm(): total = lax.psum(jnp.sum(layer_out * layer_out, axis=1), 'mp')  28 us
    dot_general x9, matrix products, block_scores(): jnp.einsum('qhd,khd->hqk', queries, key_rows.reshape(row_count, head_coun...  19.1 us
    dynamic_slice x9, local copies, waits for them, and re-layouts, add_group(): tap_row = lax.dynamic_index_in_dim(taps, tap_index, 0, keepdims=False)  15 us
    ppermute x8, local copies, waits for them, and re-layouts, shifted(): lax.ppermute(value, axis, [(source, source + steps) for source in range(f...  12.3 us
    dot_general x9, matrix products, local(): jnp.einsum('hqk,khd->qhd', weights, entry[0].reshape(row_count, head_coun...  8.19 us
  transfers between devices with their start and end apart: 27, of which 20 were waited for; matrix products, arithmetic and copies ran while one was open for 36% of the time, Pallas kernels for 0%

commit v1 on v0

v1 whole, which is shorter than its diff:
```python
import functools
import math

import jax
import jax.numpy as jnp
from jax import lax
from jax.experimental import pallas as pl
from jax.experimental.pallas import tpu as pltpu
from jax.sharding import PartitionSpec as P

D = 8192
HEAD = 128
TOK = 128
SE_K = 7
MR_K = 128
MESH = pl.DeviceIdType.MESH
F32 = jnp.float32
BF16 = jnp.bfloat16


def ring(index, step, size):
    return lax.rem(index + (step + size), size)


def kernel(
    planes,
    width,
    mps,
    d_model,
    se_q,
    se_k,
    se_v,
    mr_q,
    mr_k,
    att_q,
    att_k,
    ids,
    se_taps,
    mr_taps,
    rates,
    se_gain,
    mr_gain,
    att_gain,
    mr_out,
    att_out,
    ue,
    ybuf,
    filt,
    idc,
    m7,
    ma,
    mb,
    um,
    ul,
    sq,
    sh_send,
    sh_recv,
    v_send,
    v_recv,
    r_send,
    r_recv,
    ps_send,
    ps_recv,
    id_send,
    id_prev,
    id_all,
    k_all,
    q_all,
    v_all,
    s_buf,
    p_all,
    linv,
    o_send,
    o_all,
    loc_sem,
    k_ss,
    k_rs,
    q_ss,
    q_rs,
    v_ss,
    v_rs,
    o_ss,
    o_rs,
    i_ss,
    i_rs,
    f_ss,
    f_rs,
    ps_ss,
    ps_rs,
    h_ss,
    h_rs,
):
    seq = lax.axis_index("seq")
    mp = lax.axis_index("mp")
    count = planes * width
    z = seq // width
    w = lax.rem(seq, width)
    chans = se_q.shape[1]
    groups = chans // 128
    cw = chans // width
    heads = cw // HEAD
    span = width + 1

    def mate(step):
        return z * width + ring(w, step, width)

    def remote(src, dst, ss, rs, where):
        return pltpu.make_async_remote_copy(
            src_ref=src, dst_ref=dst, send_sem=ss, recv_sem=rs, device_id=where, device_id_type=MESH
        )

    def lanes(g, size=128):
        return pl.ds(pl.multiple_of(g * size, 128), size)

    next_seq = {"seq": ring(seq, 1, count)}
    next_plane = {"seq": ring(seq, width, count)}

    barrier = pltpu.get_barrier_semaphore()
    for step in range(1, width):
        pl.semaphore_signal(barrier, inc=1, device_id={"seq": mate(step)}, device_id_type=MESH)
    pl.semaphore_signal(barrier, inc=1, device_id={"seq": ring(seq, -width, count)}, device_id_type=MESH)
    pl.semaphore_signal(barrier, inc=1, device_id={"seq": ring(seq, -1, count)}, device_id_type=MESH)
    for step in range(1, mps):
        pl.semaphore_signal(barrier, inc=1, device_id={"mp": ring(mp, step, mps)}, device_id_type=MESH)

    own_k = pltpu.make_async_copy(att_k.at[:, lanes(w, cw)], k_all.at[width + w], loc_sem.at[0])
    own_q = pltpu.make_async_copy(att_q.at[:, lanes(w, cw)], q_all.at[w], loc_sem.at[1])
    own_k.start()
    own_q.start()

    id_row = ids[...].astype(F32)
    id_send[...] = jnp.broadcast_to(id_row, (8, 128))
    id_all[width + w] = jnp.broadcast_to(id_row, (8, 128))
    idc[TOK:] = jnp.broadcast_to(id_row, (TOK, 128)).T
    sh_send[...] = (se_k[TOK - 16 :, :].astype(F32) * se_v[TOK - 16 :, :].astype(F32)).astype(BF16)

    pl.semaphore_wait(barrier, (width - 1) + 2 + (mps - 1))

    id_next = remote(id_send, id_prev, h_ss.at[0], h_rs.at[0], next_seq)
    id_next.start()
    sh_next = remote(sh_send, sh_recv, h_ss.at[1], h_rs.at[1], next_seq)
    sh_next.start()
    sends = [id_next, sh_next]
    for step in range(1, width):
        there = ring(w, step, width)
        copy = remote(
            id_send, id_all.at[width + w], i_ss.at[step], i_rs.at[w], {"seq": mate(step)}
        )
        copy.start()
        sends.append(copy)
        copy = remote(
            att_k.at[:, lanes(there, cw)],
            k_all.at[width + w],
            k_ss.at[step],
            k_rs.at[w],
            {"seq": mate(step)},
        )
        copy.start()
        sends.append(copy)

    def local_part(g, carry):
        col = lanes(g)
        row = lax.broadcasted_iota(jnp.int32, (MR_K, 128), 0).astype(F32)
        filt[:, col] = mr_taps[:, col].astype(F32) * jnp.exp(-(rates[:, col] * row))
        ue[TOK:, col] = (
            (se_k[:, col].astype(F32) * se_v[:, col].astype(F32)).astype(BF16).astype(F32)
        )
        return carry

    lax.fori_loop(0, groups, local_part, 0)

    id_next.wait_recv()
    idc[:TOK] = jnp.broadcast_to(id_prev[0:1, :], (TOK, 128)).T
    here = idc[TOK:]
    for tap in range(1, SE_K):
        m7[tap] = (idc[TOK - tap : 2 * TOK - tap] == here).astype(F32)

    sh_next.wait_recv()
    ue[TOK - 8 : TOK, :] = sh_recv[...].astype(F32)[8:16, :]
    sq[...] = jnp.zeros_like(sq)

    def short_part(g, carry):
        col = lanes(g)
        for rb in range(TOK // 32):
            rows = slice(32 * rb, 32 * rb + 32)
            acc = ue[TOK + 32 * rb : TOK + 32 * rb + 32, col] * se_taps[0:1, col]
            for tap in range(1, SE_K):
                acc += (
                    ue[TOK + 32 * rb - tap : TOK + 32 * rb + 32 - tap, col] * m7[tap, rows, :]
                ) * se_taps[tap : tap + 1, col]
            out = se_q[rows, col].astype(F32) * acc
            sq[rows, :] += out * out
            out = out * se_gain[:, col]
            ybuf[rows, col] = out
            v_send[rows, col] = (out * mr_k[rows, col].astype(F32)).astype(BF16)
        return carry

    parts = 4
    per = groups // parts
    halo = []
    for part in range(parts):
        lax.fori_loop(part * per, (part + 1) * per, short_part, 0)
        cols = slice(part * per * 128, (part + 1) * per * 128)
        copy = remote(
            v_send.at[:, cols], v_recv.at[:, cols], h_ss.at[3 + part], h_rs.at[3 + part], next_seq
        )
        copy.start()
        halo.append(copy)
    sends += halo

    def psum_start(which):
        row = jnp.sum(sq[...].T, axis=0, keepdims=True)
        ps_send[which] = jnp.broadcast_to(row, (8, 128))
        copies = []
        for step in range(1, mps):
            copy = remote(
                ps_send.at[which],
                ps_recv.at[which, step],
                ps_ss.at[which, step],
                ps_rs.at[which, step],
                {"mp": ring(mp, step, mps)},
            )
            copy.start()
            copies.append(copy)
        return copies

    def psum_end(which, copies):
        total = ps_send[which]
        for step, copy in enumerate(copies, 1):
            copy.wait_recv()
            total = total + ps_recv[which, step]
        return lax.rsqrt(total / d_model + 1e-06)

    def column(rows8):
        return jnp.broadcast_to(rows8[0:1, :], (TOK, 128)).T

    copies = psum_start(0)
    sends += copies

    blocks = TOK // 16

    def masks(a, carry):
        base = pl.multiple_of(a * 16, 16)
        first = idc[pl.ds(base + TOK, 8), :][0:1, :]
        win = idc[pl.ds(base, TOK + 16), :]
        ma[a] = (win == first).astype(F32)
        ul[...] = idc[pl.ds(base + TOK - 16, 32), :]
        sub = lax.broadcasted_iota(jnp.int32, (8, 128), 0)
        at = 0
        for tile in range(2):
            mine = ul[16 + 8 * tile : 24 + 8 * tile, :]
            for tap in range(8 * tile + 8):
                then = ul[16 + 8 * tile - tap : 24 + 8 * tile - tap, :]
                keep = (mine == then) & (mine != first) & (sub + 8 * tile >= tap)
                mb[a, at] = keep.astype(F32)
                at += 1
        return carry

    lax.fori_loop(0, blocks, masks, 0)

    r_own = psum_end(0, copies)
    r_send[...] = r_own
    r_next = remote(r_send, r_recv, h_ss.at[2], h_rs.at[2], next_seq)
    r_next.start()
    sends.append(r_next)
    idc[:TOK] = column(r_own)

    own_k.wait()
    for step in range(1, width):
        src = ring(w, -step, width)
        remote(
            k_all.at[width + src], k_all.at[width + src], k_ss.at[step], k_rs.at[src], next_seq
        ).wait_recv()
        remote(
            id_all.at[width + src], id_all.at[width + src], i_ss.at[step], i_rs.at[src], next_seq
        ).wait_recv()
    k_next = remote(
        k_all.at[pl.ds(width, width)], k_all.at[pl.ds(0, width)], f_ss.at[width], f_rs.at[width], next_plane
    )
    k_next.start()
    i_next = remote(
        id_all.at[pl.ds(width, width)],
        id_all.at[pl.ds(0, width)],
        f_ss.at[width + 1],
        f_rs.at[width + 1],
        next_plane,
    )
    i_next.start()
    sends += [k_next, i_next]
    for step in range(1, width):
        there = ring(w, step, width)
        copy = remote(
            att_q.at[:, lanes(there, cw)], q_all.at[w], q_ss.at[step], q_rs.at[w], {"seq": mate(step)}
        )
        copy.start()
        sends.append(copy)

    r_next.wait_recv()
    idc[TOK:] = column(r_recv[...])
    for copy in halo:
        copy.wait_recv()
    sq[...] = jnp.zeros_like(sq)

    def medium_part(g, carry):
        col = lanes(g)
        se_out = (ybuf[:, col] * idc[:TOK]).astype(BF16).astype(F32)
        ue[TOK:, col] = (mr_k[:, col].astype(F32) * se_out).astype(BF16).astype(F32)
        ue[:TOK, col] = v_recv[:, col].astype(F32) * idc[TOK:]

        def block(a, carry):
            base = pl.multiple_of(a * 16, 16)
            um[...] = ue[pl.ds(base, TOK + 16), col] * ma[a]
            ul[...] = ue[pl.ds(base + TOK - 16, 32), col]
            acc = [[jnp.zeros((8, 128), F32) for _ in range(4)] for _ in range(2)]
            for phase in range(8):
                wins = {k: um[8 * k - phase : 8 * k - phase + 8, :] for k in range(1, 18)}
                for m in range(MR_K // 8):
                    tap = filt[8 * m + phase : 8 * m + phase + 1, col]
                    for tile in range(2):
                        acc[tile][phase % 4] += wins[16 + tile - m] * tap
            at = 0
            for tile in range(2):
                total = (acc[tile][0] + acc[tile][1]) + (acc[tile][2] + acc[tile][3])
                total = total * ma[a, TOK + 8 * tile : TOK + 8 * tile + 8, :]
                for tap in range(8 * tile + 8):
                    total += (ul[16 + 8 * tile - tap : 24 + 8 * tile - tap, :] * mb[a, at]) * filt[
                        tap : tap + 1, col
                    ]
                    at += 1
                um[8 * tile : 8 * tile + 8, :] = total
            rows = pl.ds(base, 16)
            out = mr_q[rows, col].astype(F32) * um[0:16, :]
            ybuf[rows, col] = out
            sq[rows, :] += out * out
            return carry

        return lax.fori_loop(0, blocks, block, carry)

    lax.fori_loop(0, groups, medium_part, 0)

    copies = psum_start(1)
    sends += copies
    r_own = psum_end(1, copies)
    idc[:TOK] = column(r_own)

    def norm_chunk(there):
        for part in range(cw // 128):
            col = lanes(there * (cw // 128) + part)
            mr_out[:, col] = (ybuf[:, col] * idc[:TOK] * mr_gain[:, col]).astype(BF16)

    for step in range(1, width):
        there = ring(w, step, width)
        norm_chunk(there)
        copy = remote(
            mr_out.at[:, lanes(there, cw)],
            v_all.at[width + w],
            v_ss.at[step],
            v_rs.at[w],
            {"seq": mate(step)},
        )
        copy.start()
        sends.append(copy)
    norm_chunk(w)
    own_v = pltpu.make_async_copy(mr_out.at[:, lanes(w, cw)], v_all.at[width + w], loc_sem.at[2])
    own_v.start()

    own_q.wait()
    for step in range(1, width):
        src = ring(w, -step, width)
        remote(q_all.at[src], q_all.at[src], q_ss.at[step], q_rs.at[src], next_seq).wait_recv()
    k_next.wait_recv()
    i_next.wait_recv()

    scale = HEAD**-0.5 * math.log2(math.e)
    tri = lax.broadcasted_iota(jnp.int32, (TOK, TOK), 0) >= lax.broadcasted_iota(
        jnp.int32, (TOK, TOK), 1
    )

    def weights(b):
        id_q = column(id_all[width + b])
        for h in range(heads):
            hl = slice(h * HEAD, (h + 1) * HEAD)
            q = q_all[b, :, hl]
            top = None
            for kk in range(span):
                s = lax.dot_general(
                    q,
                    k_all[b + kk, :, hl],
                    (((1,), (1,)), ((), ())),
                    preferred_element_type=F32,
                )
                keep = id_q == jnp.broadcast_to(id_all[b + kk][0:1, :], (TOK, TOK))
                if kk == span - 1:
                    keep = keep & tri
                s = jnp.where(keep, s * scale, -1e30)
                s_buf[kk] = s
                top = s if top is None else jnp.maximum(top, s)
            top = jnp.max(top, axis=1, keepdims=True)
            total = None
            for kk in range(span):
                e = jnp.exp2(s_buf[kk] - top)
                total = e if total is None else total + e
                p_all[b, h, :, kk * TOK : (kk + 1) * TOK] = e.astype(BF16)
            total = jnp.sum(total, axis=1, keepdims=True)
            linv[b, h] = jnp.broadcast_to(1.0 / total, (TOK, TOK))

    own_v.wait()

    def weigh_and_forward(i, carry):
        weights(i)
        j = width - 1 - i

        @pl.when(j != w)
        def _():
            remote(
                v_all.at[width + j], v_all.at[width + j], v_ss.at[0], v_rs.at[j], next_seq
            ).wait_recv()

        remote(v_all.at[width + j], v_all.at[j], f_ss.at[j], f_rs.at[j], next_plane).start()
        return carry

    lax.fori_loop(0, width, weigh_and_forward, 0)

    def mix(i, carry):
        b = width - 1 - i
        remote(v_all.at[width + b], v_all.at[b], f_ss.at[b], f_rs.at[b], next_plane).wait_recv()
        for h in range(heads):
            hl = slice(h * HEAD, (h + 1) * HEAD)
            o = None
            for kk in range(span):
                term = lax.dot_general(
                    p_all[b, h, :, kk * TOK : (kk + 1) * TOK],
                    v_all[b + kk, :, hl],
                    (((1,), (0,)), ((), ())),
                    preferred_element_type=F32,
                )
                o = term if o is None else o + term
            o_send[b, :, hl] = (o * linv[b, h]).astype(BF16)

        @pl.when(b != w)
        def _():
            remote(
                o_send.at[b],
                o_all.at[w],
                o_ss.at[b],
                o_rs.at[w],
                {"seq": z * width + b},
            ).start()

        return carry

    lax.fori_loop(0, width, mix, 0)
    o_all[w] = o_send[w]
    sq[...] = jnp.zeros_like(sq)

    def collect(i, carry):
        src = ring(w, i, width)

        @pl.when(i != 0)
        def _():
            remote(o_all.at[src], o_all.at[src], o_ss.at[src], o_rs.at[src], next_seq).wait_recv()

        for part in range(cw // 128):
            out = o_all[src, :, part * 128 : (part + 1) * 128].astype(F32)
            sq[...] += out * out
        return carry

    lax.fori_loop(0, width, collect, 0)
    copies = psum_start(2)
    sends += copies
    scale_col = column(psum_end(2, copies))

    for j in range(width):
        for part in range(cw // 128):
            col = slice(j * cw + part * 128, j * cw + (part + 1) * 128)
            out = o_all[j, :, part * 128 : (part + 1) * 128].astype(F32)
            att_out[:, col] = (out * scale_col * att_gain[:, col]).astype(BF16)

    for copy in sends:
        copy.wait_send()

    def drain(j, carry):
        remote(v_all.at[width + j], v_all.at[j], f_ss.at[j], f_rs.at[j], next_plane).wait_send()

        @pl.when(j != w)
        def _():
            remote(
                o_send.at[j], o_all.at[w], o_ss.at[j], o_rs.at[w], {"seq": z * width + j}
            ).wait_send()

        return carry

    lax.fori_loop(0, width, drain, 0)


def local(planes, width, mps, d_model, *args):
    (se_q, se_k, se_v, mr_q, mr_k, att_q, att_k, ids, se_taps, mr_taps, rates, g1, g2, g3) = args
    chans = se_q.shape[1]
    cw = chans // width
    heads = cw // HEAD
    span = width + 1
    vm = pl.BlockSpec(memory_space=pltpu.VMEM)
    anyspec = pl.BlockSpec(memory_space=pl.ANY)
    vmem = pltpu.VMEM
    dma = pltpu.SemaphoreType.DMA
    out = jax.ShapeDtypeStruct((TOK, chans), BF16)
    return pl.pallas_call(
        functools.partial(kernel, planes, width, mps, d_model),
        out_shape=(out, out),
        in_specs=[vm] * 5 + [anyspec] * 2 + [vm] * 7,
        out_specs=(vm, vm),
        scratch_shapes=[
            vmem((2 * TOK, chans), F32),
            vmem((TOK, chans), F32),
            vmem((MR_K, chans), F32),
            vmem((2 * TOK, 128), F32),
            vmem((SE_K, TOK, 128), F32),
            vmem((TOK // 16, TOK + 16, 128), F32),
            vmem((TOK // 16, 24, 8, 128), F32),
            vmem((TOK + 16, 128), F32),
            vmem((32, 128), F32),
            vmem((TOK, 128), F32),
            vmem((16, chans), BF16),
            vmem((16, chans), BF16),
            vmem((TOK, chans), BF16),
            vmem((TOK, chans), BF16),
            vmem((8, 128), F32),
            vmem((8, 128), F32),
            vmem((3, 8, 128), F32),
            vmem((3, mps, 8, 128), F32),
            vmem((8, 128), F32),
            vmem((8, 128), F32),
            vmem((2 * width, 8, 128), F32),
            vmem((2 * width, TOK, cw), BF16),
            vmem((width, TOK, cw), BF16),
            vmem((2 * width, TOK, cw), BF16),
            vmem((span, TOK, TOK), F32),
            vmem((width, heads, TOK, span * TOK), BF16),
            vmem((width, heads, TOK, TOK), F32),
            vmem((width, TOK, cw), BF16),
            vmem((width, TOK, cw), BF16),
            dma((3,)),
            dma((width,)),
            dma((width,)),
            dma((width,)),
            dma((width,)),
            dma((width,)),
            dma((width,)),
            dma((width,)),
            dma((width,)),
            dma((width,)),
            dma((width,)),
            dma((width + 2,)),
            dma((width + 2,)),
            dma((3, mps)),
            dma((3, mps)),
            dma((8,)),
            dma((8,)),
        ],
        compiler_params=pltpu.CompilerParams(
            collective_id=0, has_side_effects=True, vmem_limit_bytes=48 * 1024 * 1024
        ),
    )(
        se_q,
        se_k,
        se_v,
        mr_q,
        mr_k,
        att_q,
        att_k,
        ids.reshape(1, TOK),
        se_taps,
        mr_taps,
        rates.reshape(1, chans),
        g1.reshape(1, chans),
        g2.reshape(1, chans),
        g3.reshape(1, chans),
    )


def solution(mesh, width=8, d_model=D):
    planes = mesh.shape["seq"] // width
    spec = P("seq", "mp")
    return jax.shard_map(
        functools.partial(local, planes, width, mesh.shape["mp"], d_model),
        mesh=mesh,
        in_specs=(spec,) * 7
        + (P("seq"), P(None, "mp"), P(None, "mp"), P("mp"), P("mp"), P("mp"), P("mp")),
        out_specs=(spec, spec),
        check_vma=False,
    )
```

time: 308 us -> 88.3 us (0.29)
  the two profiles are of different devices: /device:TPU:128 before, /device:TPU:6 now
where the time goes in v1:
time: 88.3 us; the launch traced here: 87.6 us
  Pallas kernels  73.4 us (83%)
  local copies, waits for them, and re-layouts  13.5 us (15%)
    pallas_call x1, Pallas kernels, local(): pl.pallas_call(functools.partial(kernel, planes, width, mps, d_model), ou...  73.4 us
    unnamed x30, local copies, waits for them, and re-layouts  13.5 us

profile of v1, /device:TPU:6, one launch (start us, length us, event | category | flops | bytes accessed | tf_op | source)
XLA Modules:
  0.0 87.6 jit_solution(3476026303810980486)
XLA Ops:
  0.6 0.0 copy-start.9
  0.6 0.0 copy-start.13
  0.7 0.7 copy-done.9
  1.3 0.0 copy-done.13
  1.3 0.0 copy-start
  1.3 1.0 %copy-done = bf16[128,2048]{1,0:T(8,128)(2,1)S(1)} copy-done((bf16[128,2048]{1,0:T(8,128)(2,1)S(1)}, bf16[128,2048]{1,0:T(8,128)(2,1)}, u32[]{:S(2)}) %copy-start) | copy-done | bytes 524312
  2.4 0.0 copy-start.1
  2.4 1.0 %copy-done.1 = bf16[128,2048]{1,0:T(8,128)(2,1)S(1)} copy-done((bf16[128,2048]{1,0:T(8,128)(2,1)S(1)}, bf16[128,2048]{1,0:T(8,128)(2,1)}, u32[]{:S(2)}) %copy-start.1) | copy-done | bytes 524312
  3.4 0.0 copy-start.2
  3.4 1.0 %copy-done.2 = bf16[128,2048]{1,0:T(8,128)(2,1)S(1)} copy-done((bf16[128,2048]{1,0:T(8,128)(2,1)S(1)}, bf16[128,2048]{1,0:T(8,128)(2,1)}, u32[]{:S(2)}) %copy-start.2) | copy-done | bytes 524312
  4.5 0.0 copy-start.3
  4.5 1.0 %copy-done.3 = bf16[128,2048]{1,0:T(8,128)(2,1)S(1)} copy-done((bf16[128,2048]{1,0:T(8,128)(2,1)S(1)}, bf16[128,2048]{1,0:T(8,128)(2,1)}, u32[]{:S(2)}) %copy-start.3) | copy-done | bytes 524312
  5.5 1.0 %copy-done.4 = bf16[128,2048]{1,0:T(8,128)(2,1)S(1)} copy-done((bf16[128,2048]{1,0:T(8,128)(2,1)S(1)}, bf16[128,2048]{1,0:T(8,128)(2,1)}, u32[]{:S(2)}) %copy-start.4) | copy-done | bytes 524312
  6.5 0.0 copy-start.5
  6.5 1.0 %copy-done.5 = bf16[128,2048]{1,0:T(8,128)(2,1)S(1)} copy-done((bf16[128,2048]{1,0:T(8,128)(2,1)S(1)}, bf16[128,2048]{1,0:T(8,128)(2,1)}, u32[]{:S(2)}) %copy-start.5) | copy-done | bytes 524312
  7.6 1.0 %copy-done.6 = bf16[128,2048]{1,0:T(8,128)(2,1)S(1)} copy-done((bf16[128,2048]{1,0:T(8,128)(2,1)S(1)}, bf16[128,2048]{1,0:T(8,128)(2,1)}, u32[]{:S(2)}) %copy-start.6) | copy-done | bytes 524312
  8.6 1.0 %copy-done.7 = bf16[128,2048]{1,0:T(8,128)(2,1)S(1)} copy-done((bf16[128,2048]{1,0:T(8,128)(2,1)S(1)}, bf16[128,2048]{1,0:T(8,128)(2,1)}, u32[]{:S(2)}) %copy-start.7) | copy-done | bytes 524312
  9.7 0.8 copy-done.8
  10.5 0.7 copy-done.10
  11.2 0.7 copy-done.11
  11.9 0.7 copy-done.12
  12.6 73.4 %shard_map.149 = (bf16[128,2048]{1,0:T(8,128)(2,1)S(1)}, bf16[128,2048]{1,0:T(8,128)(2,1)S(1)}) custom-call(bf16[128,2048]{1,0:T(8,128)(2,1)S(1)} %copy-done, bf16[128,2048]{1,0:T(8,128)(2,1)S(1)} %copy-done.1, bf16[128,2048]{1,0:T(8,128)(2,1)S(1)} %copy-done.2, bf16[128,2048]{1,0:T(8,128)(2,1)S(1)} %copy-done.3, bf16[128,2048]{1,0:T(8,128)(2,1)S(1)} %copy-done.4, ...), custom_call_target="tpu_custom_call" | custom-call | tf_op jit(solution)/shard_map/pallas_call | solution.py:507
  86.0 0.8 copy.18
  86.8 0.8 copy.19
  (7 shorter events, 0.0 us)
Async XLA Ops:
  0.6 0.7 copy-start.9
  0.6 0.7 copy-start.13
  1.3 1.0 %copy-start = (bf16[128,2048]{1,0:T(8,128)(2,1)S(1)}, bf16[128,2048]{1,0:T(8,128)(2,1)}, u32[]{:S(2)}) copy-start(bf16[128,2048]{1,0:T(8,128)(2,1)} %se_q.1) | copy-start | bytes 1572868
  2.4 1.0 %copy-start.1 = (bf16[128,2048]{1,0:T(8,128)(2,1)S(1)}, bf16[128,2048]{1,0:T(8,128)(2,1)}, u32[]{:S(2)}) copy-start(bf16[128,2048]{1,0:T(8,128)(2,1)} %se_k.1) | copy-start | bytes 1572868
  3.4 1.0 %copy-start.2 = (bf16[128,2048]{1,0:T(8,128)(2,1)S(1)}, bf16[128,2048]{1,0:T(8,128)(2,1)}, u32[]{:S(2)}) copy-start(bf16[128,2048]{1,0:T(8,128)(2,1)} %se_v.1) | copy-start | bytes 1572868
  4.5 1.0 %copy-start.3 = (bf16[128,2048]{1,0:T(8,128)(2,1)S(1)}, bf16[128,2048]{1,0:T(8,128)(2,1)}, u32[]{:S(2)}) copy-start(bf16[128,2048]{1,0:T(8,128)(2,1)} %mr_q.1) | copy-start | bytes 1572868
  5.5 1.0 %copy-start.4 = (bf16[128,2048]{1,0:T(8,128)(2,1)S(1)}, bf16[128,2048]{1,0:T(8,128)(2,1)}, u32[]{:S(2)}) copy-start(bf16[128,2048]{1,0:T(8,128)(2,1)} %mr_k.1) | copy-start | bytes 1572868
  6.5 1.0 %copy-start.5 = (bf16[128,2048]{1,0:T(8,128)(2,1)S(1)}, bf16[128,2048]{1,0:T(8,128)(2,1)}, u32[]{:S(2)}) copy-start(bf16[128,2048]{1,0:T(8,128)(2,1)} %att_q.1) | copy-start | bytes 1572868
  7.6 1.0 %copy-start.6 = (bf16[128,2048]{1,0:T(8,128)(2,1)S(1)}, bf16[128,2048]{1,0:T(8,128)(2,1)}, u32[]{:S(2)}) copy-start(bf16[128,2048]{1,0:T(8,128)(2,1)} %att_k.1) | copy-start | bytes 1572868
  8.6 1.0 %copy-start.7 = (bf16[128,2048]{1,0:T(8,128)(2,1)S(1)}, bf16[128,2048]{1,0:T(8,128)(2,1)}, u32[]{:S(2)}) copy-start(bf16[128,2048]{1,0:T(8,128)(2,1)} %mr_taps.1) | copy-start | bytes 1572868
  9.7 0.8 copy-start.8
  10.5 0.7 copy-start.10
  11.2 0.7 copy-start.11
  11.9 0.7 copy-start.12

commit v2 on v1

v2 whole, which is shorter than its diff:
```python
import functools
import math

import jax
import jax.numpy as jnp
import numpy as np
from jax import lax
from jax.experimental import pallas as pl
from jax.experimental.pallas import tpu as pltpu
from jax.sharding import PartitionSpec as P

D = 8192
HEAD = 128
TOK = 128
SE_K = 7
MR_K = 128
MESH = pl.DeviceIdType.MESH
F32 = jnp.float32
BF16 = jnp.bfloat16


def transforms(n):
    k = np.arange(n)[:, None]
    t = np.arange(n)[None, :]
    cos, sin = np.cos(np.pi * k * t / n), np.sin(np.pi * k * t / n)
    sin[0] = np.cos(np.pi * t[0])
    forth = np.concatenate([cos, sin], 0)
    t = t + n
    cos, sin = np.cos(np.pi * k * t / n), np.sin(np.pi * k * t / n)
    sin[0] = np.cos(np.pi * t[0])
    back = np.concatenate([cos, sin], 0) / n
    back[0] /= 2
    back[n] /= 2
    return jnp.asarray(forth, BF16), jnp.asarray(back.T, BF16)


def ring(index, step, size):
    return lax.rem(index + (step + size), size)


def kernel(
    planes,
    width,
    mps,
    d_model,
    se_q_h,
    se_k_h,
    se_v_h,
    mr_q_h,
    mr_k_h,
    att_q,
    att_k,
    ids_h,
    se_taps_h,
    mr_taps_h,
    rates_h,
    se_gain_h,
    mr_gain_h,
    att_gain_h,
    forth_h,
    back_h,
    mr_out,
    att_out,
    se_q,
    se_k,
    se_v,
    mr_q,
    mr_k,
    ids,
    se_taps,
    mr_taps,
    rates,
    se_gain,
    mr_gain,
    att_gain,
    forth,
    back,
    in_sem,
    ue,
    ybuf,
    filt,
    idc,
    m7,
    ma,
    mb,
    um,
    ul,
    sq,
    sh_send,
    sh_recv,
    v_send,
    v_recv,
    r_send,
    r_recv,
    ps_send,
    ps_recv,
    id_send,
    id_prev,
    id_all,
    k_all,
    q_all,
    v_all,
    s_buf,
    p_all,
    linv,
    v_raw,
    v_s,
    hat_a,
    hat_b,
    hat_c,
    hat,
    hat_y,
    u_in,
    m_prior,
    r_col,
    o_acc,
    t_val,
    t_val2,
    t_all,
    r_val,
    r_all,
    o_send,
    o_all,
    loc_sem,
    k_ss,
    k_rs,
    q_ss,
    q_rs,
    v_ss,
    v_rs,
    o_ss,
    o_rs,
    i_ss,
    i_rs,
    f_ss,
    f_rs,
    g_ss,
    g_rs,
    t_ss,
    t_rs,
    ps_ss,
    ps_rs,
    h_ss,
    h_rs,
):
    seq = lax.axis_index("seq")
    mp = lax.axis_index("mp")
    count = planes * width
    z = seq // width
    w = lax.rem(seq, width)
    chans = se_q.shape[1]
    groups = chans // 128
    cw = chans // width
    heads = cw // HEAD
    span = width + 1

    def mate(step):
        return z * width + ring(w, step, width)

    def remote(src, dst, ss, rs, where):
        return pltpu.make_async_remote_copy(
            src_ref=src, dst_ref=dst, send_sem=ss, recv_sem=rs, device_id=where, device_id_type=MESH
        )

    def lanes(g, size=128):
        return pl.ds(pl.multiple_of(g * size, 128), size)

    next_seq = {"seq": ring(seq, 1, count)}
    next_plane = {"seq": ring(seq, width, count)}

    barrier = pltpu.get_barrier_semaphore()
    for step in range(1, width):
        pl.semaphore_signal(barrier, inc=1, device_id={"seq": mate(step)}, device_id_type=MESH)
    for there in range(width):
        pl.semaphore_signal(
            barrier,
            inc=1,
            device_id={"seq": ring(z, -1, planes) * width + there},
            device_id_type=MESH,
        )
    pl.semaphore_signal(barrier, inc=1, device_id={"seq": ring(seq, -1, count)}, device_id_type=MESH)
    for step in range(1, mps):
        pl.semaphore_signal(barrier, inc=1, device_id={"mp": ring(mp, step, mps)}, device_id_type=MESH)

    loads = {}
    for src, dst in (
        (ids_h, ids),
        (se_k_h, se_k),
        (se_v_h, se_v),
        (mr_taps_h, mr_taps),
        (rates_h, rates),
        (forth_h, forth),
        (se_q_h, se_q),
        (mr_k_h, mr_k),
        (se_taps_h, se_taps),
        (se_gain_h, se_gain),
        (mr_q_h, mr_q),
        (mr_gain_h, mr_gain),
        (att_gain_h, att_gain),
        (back_h, back),
    ):
        copy = pltpu.make_async_copy(src, dst, in_sem.at[len(loads)])
        copy.start()
        loads[id(dst)] = copy

    def loaded(*refs):
        for ref in refs:
            loads[id(ref)].wait()

    own_k = pltpu.make_async_copy(att_k.at[:, lanes(w, cw)], k_all.at[width + w], loc_sem.at[0])
    own_q = pltpu.make_async_copy(att_q.at[:, lanes(w, cw)], q_all.at[w], loc_sem.at[1])
    own_k.start()
    own_q.start()

    loaded(ids)
    id_row = ids[...].astype(F32)
    id_send[...] = jnp.broadcast_to(id_row, (8, 128))
    id_all[width + w] = jnp.broadcast_to(id_row, (8, 128))
    idc[TOK:] = jnp.broadcast_to(id_row, (TOK, 128)).T
    loaded(se_k, se_v)
    sh_send[...] = (se_k[TOK - 16 :, :].astype(F32) * se_v[TOK - 16 :, :].astype(F32)).astype(BF16)

    def local_part(g, carry):
        col = lanes(g)
        row = lax.broadcasted_iota(jnp.int32, (MR_K, 128), 0).astype(F32)
        filt[:, col] = mr_taps[:, col].astype(F32) * jnp.exp(-(rates[:, col] * row))
        ue[TOK:, col] = (
            (se_k[:, col].astype(F32) * se_v[:, col].astype(F32)).astype(BF16).astype(F32)
        )
        return carry

    def filter_part(g, carry):
        col = lanes(g, 256)
        full = filt[:, col]
        high = full.astype(BF16)
        low = (full - high.astype(F32)).astype(BF16)
        hat = jnp.dot(forth[...], high, preferred_element_type=F32) + jnp.dot(
            forth[...], low, preferred_element_type=F32
        )
        top = lax.broadcasted_iota(jnp.int32, (TOK, 256), 0) == 0
        hat_a[:, col] = hat[:TOK]
        hat_b[:, col] = jnp.where(top, 0.0, hat[TOK:])
        hat_c[:, col] = jnp.where(top, hat[TOK:], hat[:TOK])
        return carry

    loaded(mr_taps, rates, forth)
    lax.fori_loop(0, groups, local_part, 0)
    lax.fori_loop(0, groups // 2, filter_part, 0)
    idc[:TOK] = jnp.full((TOK, 128), -1.0, F32)
    ue[TOK - 8 : TOK, :] = jnp.zeros((8, chans), F32)
    here = idc[TOK:]
    for tap in range(1, SE_K):
        m7[tap] = (idc[TOK - tap : 2 * TOK - tap] == here).astype(F32)
    sq[...] = jnp.zeros_like(sq)

    def short_rows(start, size, col):
        rows = slice(start, start + size)
        acc = ue[TOK + start : TOK + start + size, col] * se_taps[0:1, col]
        for tap in range(1, SE_K):
            acc += (ue[TOK + start - tap : TOK + start + size - tap, col] * m7[tap, rows, :]) * se_taps[
                tap : tap + 1, col
            ]
        out = se_q[rows, col].astype(F32) * acc
        sq[rows, :] += out * out
        out = out * se_gain[:, col]
        ybuf[rows, col] = out
        v_send[rows, col] = (out * mr_k[rows, col].astype(F32)).astype(BF16)

    def short_part(g, carry):
        for rb in range(TOK // 32):
            short_rows(32 * rb, 32, lanes(g))
        return carry

    blocks = TOK // 16

    def masks(a, carry):
        base = pl.multiple_of(a * 16, 16)
        first = idc[pl.ds(base + TOK, 8), :][0:1, :]
        ma[a] = (idc[TOK:, :] == first).astype(F32)
        ul[...] = idc[pl.ds(base + TOK - 16, 32), :]
        sub = lax.broadcasted_iota(jnp.int32, (8, 128), 0)
        at = 0
        for tile in range(2):
            mine = ul[16 + 8 * tile : 24 + 8 * tile, :]
            for tap in range(8 * tile + 8):
                then = ul[16 + 8 * tile - tap : 24 + 8 * tile - tap, :]
                keep = (mine == then) & (mine != first) & (sub + 8 * tile >= tap)
                mb[a, at] = keep.astype(F32)
                at += 1
        return carry

    lax.fori_loop(0, blocks, masks, 0)
    um[...] = jnp.zeros_like(um)

    loaded(se_q, mr_k, se_taps, se_gain)
    lax.fori_loop(0, groups, short_part, 0)

    pl.semaphore_wait(barrier, (width - 1) + width + 1 + (mps - 1))

    id_next = remote(id_send, id_prev, h_ss.at[0], h_rs.at[0], next_seq)
    id_next.start()
    sh_next = remote(sh_send, sh_recv, h_ss.at[1], h_rs.at[1], next_seq)
    sh_next.start()
    sends = [id_next, sh_next]
    halo = [
        remote(v_send.at[rows], v_recv.at[rows], h_ss.at[at], h_rs.at[at], next_seq)
        for at, rows in ((3, pl.ds(16, TOK - 16)), (4, pl.ds(0, 16)))
    ]
    sends += halo
    for step in range(1, width):
        there = ring(w, step, width)
        copy = remote(
            id_send, id_all.at[width + w], i_ss.at[step], i_rs.at[w], {"seq": mate(step)}
        )
        copy.start()
        sends.append(copy)
        copy = remote(
            att_k.at[:, lanes(there, cw)],
            k_all.at[width + w],
            k_ss.at[step],
            k_rs.at[w],
            {"seq": mate(step)},
        )
        copy.start()
        sends.append(copy)

    halo[0].start()

    id_next.wait_recv()
    idc[:TOK] = jnp.broadcast_to(id_prev[0:1, :], (TOK, 128)).T
    for tap in range(1, SE_K):
        m7[tap, 0:16] = (idc[TOK - tap : TOK + 16 - tap] == idc[TOK : TOK + 16]).astype(F32)
    sh_next.wait_recv()
    ue[TOK - 8 : TOK, :] = sh_recv[...].astype(F32)[8:16, :]
    sq[0:16, :] = jnp.zeros((16, 128), F32)

    def first_rows(g, carry):
        short_rows(0, 16, lanes(g))
        return carry

    lax.fori_loop(0, groups, first_rows, 0)
    halo[1].start()

    def psum_start(which):
        row = jnp.sum(sq[...].T, axis=0, keepdims=True)
        ps_send[which] = jnp.broadcast_to(row, (8, 128))
        copies = []
        for step in range(1, mps):
            copy = remote(
                ps_send.at[which],
                ps_recv.at[which, step],
                ps_ss.at[which, step],
                ps_rs.at[which, step],
                {"mp": ring(mp, step, mps)},
            )
            copy.start()
            copies.append(copy)
        return copies

    def psum_end(which, copies):
        total = ps_send[which]
        for step, copy in enumerate(copies, 1):
            copy.wait_recv()
            total = total + ps_recv[which, step]
        return lax.rsqrt(total / d_model + 1e-06)

    def column(rows8):
        return jnp.broadcast_to(rows8[0:1, :], (TOK, 128)).T

    copies = psum_start(0)
    sends += copies

    m_prior[...] = (idc[:TOK] == idc[TOK : TOK + 1, :]).astype(F32)
    r_own = psum_end(0, copies)
    r_send[...] = r_own
    r_next = remote(r_send, r_recv, h_ss.at[2], h_rs.at[2], next_seq)
    r_next.start()
    sends.append(r_next)
    r_col[...] = column(r_own)

    def medium_part(g, carry):
        col = lanes(g)
        se_out = (ybuf[:, col] * r_col[...]).astype(BF16).astype(F32)
        ue[TOK:, col] = (mr_k[:, col].astype(F32) * se_out).astype(BF16).astype(F32)
        for a in range(blocks):
            size = 16 * a + 16
            base = 16 * a
            win = um.at[a % 2]
            win[8 : 8 + size, :] = ue[TOK : TOK + size, col] * ma[a, 0:size, :]
            acc = [[jnp.zeros((8, 128), F32) for _ in range(4)] for _ in range(2)]
            for phase in range(8):
                wins = [win[8 + 8 * k - phase : 16 + 8 * k - phase, :] for k in range(2 * a + 2)]
                for m in range(2 * a + 2):
                    tap = filt[8 * m + phase : 8 * m + phase + 1, col]
                    for tile in range(2):
                        if 2 * a + tile >= m:
                            acc[tile][phase % 4] += wins[2 * a + tile - m] * tap
            at = 0
            for tile in range(2):
                row = base + 8 * tile
                total = (acc[tile][0] + acc[tile][1]) + (acc[tile][2] + acc[tile][3])
                total = total * ma[a, row : row + 8, :]
                for tap in range(8 * tile + 8):
                    total += (
                        ue[TOK + row - tap : TOK + row + 8 - tap, col] * mb[a, at]
                    ) * filt[tap : tap + 1, col]
                    at += 1
                ybuf[row : row + 8, col] = total
        return carry

    lax.fori_loop(0, groups * 3 // 8, medium_part, 0)

    own_k.wait()
    for step in range(1, width):
        src = ring(w, -step, width)
        remote(
            k_all.at[width + src], k_all.at[width + src], k_ss.at[step], k_rs.at[src], next_seq
        ).wait_recv()
        remote(
            id_all.at[width + src], id_all.at[width + src], i_ss.at[step], i_rs.at[src], next_seq
        ).wait_recv()
    k_next = remote(
        k_all.at[pl.ds(width, width)], k_all.at[pl.ds(0, width)], f_ss.at[width], f_rs.at[width], next_plane
    )
    k_next.start()
    i_next = remote(
        id_all.at[pl.ds(width, width)],
        id_all.at[pl.ds(0, width)],
        f_ss.at[width + 1],
        f_rs.at[width + 1],
        next_plane,
    )
    i_next.start()
    sends += [k_next, i_next]

    lax.fori_loop(groups * 3 // 8, groups, medium_part, 0)

    loaded(mr_q, mr_gain, att_gain, back)
    r_next.wait_recv()
    r_col[...] = column(r_recv[...]) * m_prior[...]
    for copy in halo:
        copy.wait_recv()
    for step in range(1, width):
        there = ring(w, step, width)
        copy = remote(
            att_q.at[:, lanes(there, cw)], q_all.at[w], q_ss.at[step], q_rs.at[w], {"seq": mate(step)}
        )
        copy.start()
        sends.append(copy)
    sq[...] = jnp.zeros_like(sq)

    def prior_part(g, carry):
        wide = lanes(g, 256)
        halves = [lanes(2 * g + half) for half in range(2)]
        factor = r_col[...]
        for half, col in enumerate(halves):
            u_in[:, 128 * half : 128 * half + 128] = (v_recv[:, col].astype(F32) * factor).astype(BF16)
        hat[...] = jnp.dot(forth[...], u_in[...], preferred_element_type=F32)
        hat_y[:TOK, :] = (hat[:TOK] * hat_a[:, wide] - hat[TOK:] * hat_b[:, wide]).astype(BF16)
        hat_y[TOK:, :] = (hat[:TOK] * hat_b[:, wide] + hat[TOK:] * hat_c[:, wide]).astype(BF16)
        prior = jnp.dot(back[...], hat_y[...], preferred_element_type=F32)
        keep = ma[0]
        for half, col in enumerate(halves):
            out = ybuf[:, col] + keep * prior[:, 128 * half : 128 * half + 128]
            out = mr_q[:, col].astype(F32) * out
            ybuf[:, col] = out
            sq[...] += out * out
        return carry

    lax.fori_loop(0, groups // 2, prior_part, 0)

    copies = psum_start(1)
    sends += copies

    def raw_chunk(there):
        for part in range(cw // 128):
            col = lanes(there * (cw // 128) + part)
            v_raw[:, col] = (ybuf[:, col] * mr_gain[:, col]).astype(BF16)

    above = ring(z, 1, planes) * width
    for step in range(width):
        there = ring(w, step, width)
        chunk = v_raw.at[:, lanes(there, cw)]
        raw_chunk(there)
        if step > 0:
            copy = remote(chunk, v_all.at[width + w], v_ss.at[step], v_rs.at[w], {"seq": mate(step)})
            copy.start()
            sends.append(copy)
        copy = remote(chunk, v_all.at[w], f_ss.at[step], f_rs.at[w], {"seq": above + there})
        copy.start()
        sends.append(copy)
    own_v = pltpu.make_async_copy(v_raw.at[:, lanes(w, cw)], v_all.at[width + w], loc_sem.at[2])
    own_v.start()

    r_own = psum_end(1, copies)
    r_val[...] = r_own
    r_all[width + w] = r_own
    for step in range(width):
        there = ring(w, step, width)
        if step > 0:
            copy = remote(
                r_val, r_all.at[width + w], g_ss.at[step], g_rs.at[width + w], {"seq": mate(step)}
            )
            copy.start()
            sends.append(copy)
        copy = remote(
            r_val, r_all.at[w], g_ss.at[width + step], g_rs.at[w], {"seq": above + there}
        )
        copy.start()
        sends.append(copy)
    r_col[...] = column(r_own)

    own_q.wait()
    for step in range(1, width):
        src = ring(w, -step, width)
        remote(q_all.at[src], q_all.at[src], q_ss.at[step], q_rs.at[src], next_seq).wait_recv()
    k_next.wait_recv()
    i_next.wait_recv()

    scale = HEAD**-0.5 * math.log2(math.e)
    tri = lax.broadcasted_iota(jnp.int32, (TOK, TOK), 0) >= lax.broadcasted_iota(
        jnp.int32, (TOK, TOK), 1
    )

    def weights(b):
        id_q = column(id_all[width + b])
        for h in range(heads):
            hl = slice(h * HEAD, (h + 1) * HEAD)
            q = q_all[b, :, hl]
            top = None
            for kk in range(span):
                s = lax.dot_general(
                    q,
                    k_all[b + kk, :, hl],
                    (((1,), (1,)), ((), ())),
                    preferred_element_type=F32,
                )
                keep = id_q == jnp.broadcast_to(id_all[b + kk][0:1, :], (TOK, TOK))
                if kk == span - 1:
                    keep = keep & tri
                s = jnp.where(keep, s * scale, -1e30)
                s_buf[kk] = s
                top = s if top is None else jnp.maximum(top, s)
            top = jnp.max(top, axis=1, keepdims=True)
            total = None
            for kk in range(span):
                e = jnp.exp2(s_buf[kk] - top)
                total = e if total is None else total + e
                p_all[b, h, :, kk * TOK : (kk + 1) * TOK] = e.astype(BF16)
            total = jnp.sum(total, axis=1, keepdims=True)
            linv[b, h] = jnp.broadcast_to(1.0 / total, (TOK, TOK))

    def weigh(i, carry):
        weights(i)
        return carry

    lax.fori_loop(0, width, weigh, 0)

    def norm_out(g, carry):
        col = lanes(g)
        mr_out[:, col] = (ybuf[:, col] * r_col[...] * mr_gain[:, col]).astype(BF16)
        return carry

    lax.fori_loop(0, groups, norm_out, 0)

    def scale_values(slot):
        factor = column(r_all[slot])
        for part in range(cw // 128):
            col = slice(part * 128, (part + 1) * 128)
            v_s[slot, :, col] = (v_all[slot, :, col].astype(F32) * factor).astype(BF16)

    own_v.wait()

    def take_own(i, carry):
        src = ring(w, -i, width)
        slot = width + src

        @pl.when(i != 0)
        def _():
            remote(v_all.at[slot], v_all.at[slot], v_ss.at[0], v_rs.at[src], next_seq).wait_recv()
            remote(r_all.at[slot], r_all.at[slot], g_ss.at[0], g_rs.at[slot], next_seq).wait_recv()

        scale_values(slot)
        return carry

    lax.fori_loop(0, width, take_own, 0)

    for b in range(width):
        for h in range(heads):
            hl = slice(h * HEAD, (h + 1) * HEAD)
            o_acc[b, h] = jnp.dot(
                p_all[b, h, :, (width - b) * TOK :],
                v_s[width : width + b + 1, :, hl].reshape((b + 1) * TOK, HEAD),
                preferred_element_type=F32,
            )

    for b in range(width - 1, -1, -1):
        remote(v_all.at[b], v_all.at[b], v_ss.at[0], f_rs.at[b], next_seq).wait_recv()
        remote(r_all.at[b], r_all.at[b], g_ss.at[0], g_rs.at[b], next_seq).wait_recv()
        scale_values(b)
        squares = None
        for h in range(heads):
            hl = slice(h * HEAD, (h + 1) * HEAD)
            o = o_acc[b, h] + jnp.dot(
                p_all[b, h, :, : (width - b) * TOK],
                v_s[b:width, :, hl].reshape((width - b) * TOK, HEAD),
                preferred_element_type=F32,
            )
            o = o * linv[b, h]
            o_send[b, :, hl] = o.astype(BF16)
            squares = o * o if squares is None else squares + o * o

        @pl.when(w != b)
        def _():
            remote(
                o_send.at[b],
                o_all.at[w],
                o_ss.at[b],
                o_rs.at[w],
                {"seq": z * width + b},
            ).start()

        ps_send[2, b : b + 1, :] = jnp.sum(squares.T, axis=0, keepdims=True)

    copies = []
    for step in range(1, mps):
        copy = remote(
            ps_send.at[2],
            ps_recv.at[2, step],
            ps_ss.at[2, step],
            ps_rs.at[2, step],
            {"mp": ring(mp, step, mps)},
        )
        copy.start()
        copies.append(copy)
    sends += copies
    o_all[w] = o_send[w]
    total = ps_send[2]
    for step, copy in enumerate(copies, 1):
        copy.wait_recv()
        total = total + ps_recv[2, step]
    t_val[...] = total
    t_all[w] = total
    for step in range(1, width):
        copy = remote(t_val, t_all.at[w], t_ss.at[step], t_rs.at[w], {"seq": mate(step)})
        copy.start()
        sends.append(copy)

    def collect(i, total):
        src = ring(w, i, width)

        @pl.when(i != 0)
        def _():
            remote(t_all.at[src], t_all.at[src], t_ss.at[0], t_rs.at[src], next_seq).wait_recv()

        return total + t_all[src]

    t_val2[...] = lax.fori_loop(0, width, collect, jnp.zeros((8, 128), F32))
    mine = t_val2[pl.ds(w, 1), :]
    scale_col = jnp.broadcast_to(lax.rsqrt(mine / d_model + 1e-06), (TOK, 128)).T

    def finish(i, carry):
        src = ring(w, i, width)

        @pl.when(i != 0)
        def _():
            remote(o_all.at[src], o_all.at[src], o_ss.at[src], o_rs.at[src], next_seq).wait_recv()

        for part in range(cw // 128):
            col = lanes(src * (cw // 128) + part)
            out = o_all[src, :, part * 128 : (part + 1) * 128].astype(F32)
            att_out[:, col] = (out * scale_col * att_gain[:, col]).astype(BF16)
        return carry

    lax.fori_loop(0, width, finish, 0)

    for copy in sends:
        copy.wait_send()

    def drain(j, carry):
        @pl.when(j != w)
        def _():
            remote(
                o_send.at[j], o_all.at[w], o_ss.at[j], o_rs.at[w], {"seq": z * width + j}
            ).wait_send()

        return carry

    lax.fori_loop(0, width, drain, 0)


def local(planes, width, mps, d_model, *args):
    (se_q, se_k, se_v, mr_q, mr_k, att_q, att_k, ids, se_taps, mr_taps, rates, g1, g2, g3) = args
    chans = se_q.shape[1]
    cw = chans // width
    heads = cw // HEAD
    span = width + 1
    vm = pl.BlockSpec(memory_space=pltpu.VMEM)
    hbm = pl.BlockSpec(memory_space=pl.ANY)
    vmem = pltpu.VMEM
    dma = pltpu.SemaphoreType.DMA
    out = jax.ShapeDtypeStruct((TOK, chans), BF16)
    return pl.pallas_call(
        functools.partial(kernel, planes, width, mps, d_model),
        out_shape=(out, out),
        in_specs=[hbm] * 16,
        out_specs=(vm, vm),
        scratch_shapes=[
            vmem((TOK, chans), BF16),
            vmem((TOK, chans), BF16),
            vmem((TOK, chans), BF16),
            vmem((TOK, chans), BF16),
            vmem((TOK, chans), BF16),
            vmem((1, TOK), jnp.int32),
            vmem((SE_K, chans), F32),
            vmem((MR_K, chans), BF16),
            vmem((1, chans), F32),
            vmem((1, chans), F32),
            vmem((1, chans), F32),
            vmem((1, chans), F32),
            vmem((2 * TOK, TOK), BF16),
            vmem((TOK, 2 * TOK), BF16),
            dma((14,)),
            vmem((2 * TOK, chans), F32),
            vmem((TOK, chans), F32),
            vmem((MR_K, chans), F32),
            vmem((2 * TOK, 128), F32),
            vmem((SE_K, TOK, 128), F32),
            vmem((TOK // 16, TOK, 128), F32),
            vmem((TOK // 16, 24, 8, 128), F32),
            vmem((2, TOK + 8, 128), F32),
            vmem((32, 128), F32),
            vmem((TOK, 128), F32),
            vmem((16, chans), BF16),
            vmem((16, chans), BF16),
            vmem((TOK, chans), BF16),
            vmem((TOK, chans), BF16),
            vmem((8, 128), F32),
            vmem((8, 128), F32),
            vmem((3, 8, 128), F32),
            vmem((3, mps, 8, 128), F32),
            vmem((8, 128), F32),
            vmem((8, 128), F32),
            vmem((2 * width, 8, 128), F32),
            vmem((2 * width, TOK, cw), BF16),
            vmem((width, TOK, cw), BF16),
            vmem((2 * width, TOK, cw), BF16),
            vmem((span, TOK, TOK), F32),
            vmem((width, heads, TOK, span * TOK), BF16),
            vmem((width, heads, TOK, TOK), F32),
            vmem((TOK, chans), BF16),
            vmem((2 * width, TOK, cw), BF16),
            vmem((TOK, chans), F32),
            vmem((TOK, chans), F32),
            vmem((TOK, chans), F32),
            vmem((2 * TOK, 256), F32),
            vmem((2 * TOK, 256), BF16),
            vmem((TOK, 256), BF16),
            vmem((TOK, 128), F32),
            vmem((TOK, 128), F32),
            vmem((width, heads, TOK, HEAD), F32),
            vmem((8, 128), F32),
            vmem((8, 128), F32),
            vmem((width, 8, 128), F32),
            vmem((8, 128), F32),
            vmem((2 * width, 8, 128), F32),
            vmem((width, TOK, cw), BF16),
            vmem((width, TOK, cw), BF16),
            dma((3,)),
            dma((width,)),
            dma((width,)),
            dma((width,)),
            dma((width,)),
            dma((width,)),
            dma((width,)),
            dma((width,)),
            dma((width,)),
            dma((width,)),
            dma((width,)),
            dma((width + 2,)),
            dma((width + 2,)),
            dma((2 * width,)),
            dma((2 * width,)),
            dma((width,)),
            dma((width,)),
            dma((3, mps)),
            dma((3, mps)),
            dma((8,)),
            dma((8,)),
        ],
        compiler_params=pltpu.CompilerParams(
            collective_id=0, has_side_effects=True, vmem_limit_bytes=60 * 1024 * 1024
        ),
    )(
        se_q,
        se_k,
        se_v,
        mr_q,
        mr_k,
        att_q,
        att_k,
        ids.reshape(1, TOK),
        se_taps,
        mr_taps,
        rates.reshape(1, chans),
        g1.reshape(1, chans),
        g2.reshape(1, chans),
        g3.reshape(1, chans),
        *transforms(TOK),
    )


def solution(mesh, width=8, d_model=D):
    planes = mesh.shape["seq"] // width
    spec = P("seq", "mp")
    return jax.shard_map(
        functools.partial(local, planes, width, mesh.shape["mp"], d_model),
        mesh=mesh,
        in_specs=(spec,) * 7
        + (P("seq"), P(None, "mp"), P(None, "mp"), P("mp"), P("mp"), P("mp"), P("mp")),
        out_specs=(spec, spec),
        check_vma=False,
    )
```

time: 88.3 us -> 70.8 us (0.80)
  the two profiles are of different devices: /device:TPU:6 before, /device:TPU:1 now
where the time goes in v2:
time: 70.8 us; the launch traced here: 70.7 us
  Pallas kernels  67.3 us (95%)
  local copies, waits for them, and re-layouts  2.74 us (4%)
    pallas_call x1, Pallas kernels, local(): pl.pallas_call(functools.partial(kernel, planes, width, mps, d_model), ou...  67.3 us
    unnamed x4, local copies, waits for them, and re-layouts  2.74 us

profile of v2, /device:TPU:1, one launch (start us, length us, event | category | flops | bytes accessed | tf_op | source)
XLA Modules:
  0.0 70.7 jit_solution(12884425137150127531)
XLA Ops:
  0.6 67.3 %shard_map.167 = (bf16[128,2048]{1,0:T(8,128)(2,1)}, bf16[128,2048]{1,0:T(8,128)(2,1)}) custom-call(bf16[128,2048]{1,0:T(8,128)(2,1)} %se_q_h.1, bf16[128,2048]{1,0:T(8,128)(2,1)} %se_k_h.1, bf16[128,2048]{1,0:T(8,128)(2,1)} %se_v_h.1, bf16[128,2048]{1,0:T(8,128)(2,1)} %mr_q_h.1, bf16[128,2048]{1,0:T(8,128)(2,1)} %mr_k_h.1, bf16[128,2048]{1,0:T(8,128)(2,1)} %att_q.1, ...), custom_call_target="tpu_custom_call" | custom-call | tf_op jit(solution)/shard_map/pallas_call | solution.py:703
  67.9 0.0 copy-start
  67.9 1.9 %copy.20 = bf16[128,2048]{1,0:T(8,128)(2,1)} copy(bf16[128,2048]{1,0:T(8,128)(2,1)} %get-tuple-element.4) | data formatting | bytes 1048576
  69.9 0.0 copy-done
  69.9 0.8 %copy.21 = bf16[128,2048]{1,0:T(8,128)(2,1)} copy(bf16[128,2048]{1,0:T(8,128)(2,1)S(1)} %copy-done) | data formatting | bytes 1048576
Async XLA Ops:
  67.9 2.0 %copy-start = (bf16[128,2048]{1,0:T(8,128)(2,1)S(1)}, bf16[128,2048]{1,0:T(8,128)(2,1)}, u32[]{:S(2)}) copy-start(bf16[128,2048]{1,0:T(8,128)(2,1)} %get-tuple-element.5) | copy-start | bytes 1572868

commit v3 on v2

--- a/solution.py
+++ b/solution.py
@@ -136,6 +136,12 @@
     f_rs,
     g_ss,
     g_rs,
+    kf_ss,
+    kf_rs,
+    if_ss,
+    if_rs,
+    gf_ss,
+    gf_rs,
     t_ss,
     t_rs,
     ps_ss,
@@ -171,13 +177,7 @@
     barrier = pltpu.get_barrier_semaphore()
     for step in range(1, width):
         pl.semaphore_signal(barrier, inc=1, device_id={"seq": mate(step)}, device_id_type=MESH)
-    for there in range(width):
-        pl.semaphore_signal(
-            barrier,
-            inc=1,
-            device_id={"seq": ring(z, -1, planes) * width + there},
-            device_id_type=MESH,
-        )
+    pl.semaphore_signal(barrier, inc=1, device_id={"seq": ring(seq, -width, count)}, device_id_type=MESH)
     pl.semaphore_signal(barrier, inc=1, device_id={"seq": ring(seq, -1, count)}, device_id_type=MESH)
     for step in range(1, mps):
         pl.semaphore_signal(barrier, inc=1, device_id={"mp": ring(mp, step, mps)}, device_id_type=MESH)
@@ -207,6 +207,17 @@
         for ref in refs:
             loads[id(ref)].wait()
 
+    @pl.when(z == 0)
+    def _():
+        def clear(j, carry):
+            k_all[j] = jnp.zeros((TOK, cw), BF16)
+            v_all[j] = jnp.zeros((TOK, cw), BF16)
+            r_all[j] = jnp.zeros((8, 128), F32)
+            id_all[j] = jnp.full((8, 128), -1.0, F32)
+            return carry
+
+        lax.fori_loop(0, width, clear, 0)
+
     own_k = pltpu.make_async_copy(att_k.at[:, lanes(w, cw)], k_all.at[width + w], loc_sem.at[0])
     own_q = pltpu.make_async_copy(att_q.at[:, lanes(w, cw)], q_all.at[w], loc_sem.at[1])
     own_k.start()
@@ -295,7 +306,7 @@
     loaded(se_q, mr_k, se_taps, se_gain)
     lax.fori_loop(0, groups, short_part, 0)
 
-    pl.semaphore_wait(barrier, (width - 1) + width + 1 + (mps - 1))
+    pl.semaphore_wait(barrier, (width - 1) + 2 + (mps - 1))
 
     id_next = remote(id_send, id_prev, h_ss.at[0], h_rs.at[0], next_seq)
     id_next.start()
@@ -307,6 +318,7 @@
         for at, rows in ((3, pl.ds(16, TOK - 16)), (4, pl.ds(0, 16)))
     ]
     sends += halo
+    halo[0].start()
     for step in range(1, width):
         there = ring(w, step, width)
         copy = remote(
@@ -323,8 +335,6 @@
         )
         copy.start()
         sends.append(copy)
-
-    halo[0].start()
 
     id_next.wait_recv()
     idc[:TOK] = jnp.broadcast_to(id_prev[0:1, :], (TOK, 128)).T
@@ -408,32 +418,34 @@
                 ybuf[row : row + 8, col] = total
         return carry
 
-    lax.fori_loop(0, groups * 3 // 8, medium_part, 0)
-
+    def relay_key(src):
+        return (
+            remote(k_all.at[width + src], k_all.at[src], kf_ss.at[src], kf_rs.at[src], next_plane),
+            remote(id_all.at[width + src], id_all.at[src], if_ss.at[src], if_rs.at[src], next_plane),
+        )
+
+    def medium_and_relay(g, carry):
+        medium_part(g, carry)
+        i = g - relay_from
+        src = ring(w, -i, width)
+
+        @pl.when(i != 0)
+        def _():
+            slot = width + src
+            remote(k_all.at[slot], k_all.at[slot], k_ss.at[0], k_rs.at[src], next_seq).wait_recv()
+            remote(id_all.at[slot], id_all.at[slot], i_ss.at[0], i_rs.at[src], next_seq).wait_recv()
+
+        @pl.when(z < planes - 1)
+        def _():
+            for copy in relay_key(src):
+                copy.start()
+
+        return carry
+
+    relay_from = groups - width
+    lax.fori_loop(0, relay_from, medium_part, 0)
     own_k.wait()
-    for step in range(1, width):
-        src = ring(w, -step, width)
-        remote(
-            k_all.at[width + src], k_all.at[width + src], k_ss.at[step], k_rs.at[src], next_seq
-        ).wait_recv()
-        remote(
-            id_all.at[width + src], id_all.at[width + src], i_ss.at[step], i_rs.at[src], next_seq
-        ).wait_recv()
-    k_next = remote(
-        k_all.at[pl.ds(width, width)], k_all.at[pl.ds(0, width)], f_ss.at[width], f_rs.at[width], next_plane
-    )
-    k_next.start()
-    i_next = remote(
-        id_all.at[pl.ds(width, width)],
-        id_all.at[pl.ds(0, width)],
-        f_ss.at[width + 1],
-        f_rs.at[width + 1],
-        next_plane,
-    )
-    i_next.start()
-    sends += [k_next, i_next]
-
-    lax.fori_loop(groups * 3 // 8, groups, medium_part, 0)
+    lax.fori_loop(relay_from, groups, medium_and_relay, 0)
 
     loaded(mr_q, mr_gain, att_gain, back)
     r_next.wait_recv()
@@ -477,35 +489,23 @@
             col = lanes(there * (cw // 128) + part)
             v_raw[:, col] = (ybuf[:, col] * mr_gain[:, col]).astype(BF16)
 
-    above = ring(z, 1, planes) * width
-    for step in range(width):
+    for step in range(1, width):
         there = ring(w, step, width)
-        chunk = v_raw.at[:, lanes(there, cw)]
         raw_chunk(there)
-        if step > 0:
-            copy = remote(chunk, v_all.at[width + w], v_ss.at[step], v_rs.at[w], {"seq": mate(step)})
-            copy.start()
-            sends.append(copy)
-        copy = remote(chunk, v_all.at[w], f_ss.at[step], f_rs.at[w], {"seq": above + there})
+        copy = remote(
+            v_raw.at[:, lanes(there, cw)], v_all.at[width + w], v_ss.at[step], v_rs.at[w], {"seq": mate(step)}
+        )
         copy.start()
         sends.append(copy)
+    raw_chunk(w)
     own_v = pltpu.make_async_copy(v_raw.at[:, lanes(w, cw)], v_all.at[width + w], loc_sem.at[2])
     own_v.start()
 
     r_own = psum_end(1, copies)
     r_val[...] = r_own
     r_all[width + w] = r_own
-    for step in range(width):
-        there = ring(w, step, width)
-        if step > 0:
-            copy = remote(
-                r_val, r_all.at[width + w], g_ss.at[step], g_rs.at[width + w], {"seq": mate(step)}
-            )
-            copy.start()
-            sends.append(copy)
-        copy = remote(
-            r_val, r_all.at[w], g_ss.at[width + step], g_rs.at[w], {"seq": above + there}
-        )
+    for step in range(1, width):
+        copy = remote(r_val, r_all.at[width + w], g_ss.at[step], g_rs.at[w], {"seq": mate(step)})
         copy.start()
         sends.append(copy)
     r_col[...] = column(r_own)
@@ -514,8 +514,16 @@
     for step in range(1, width):
         src = ring(w, -step, width)
         remote(q_all.at[src], q_all.at[src], q_ss.at[step], q_rs.at[src], next_seq).wait_recv()
-    k_next.wait_recv()
-    i_next.wait_recv()
+
+    def take_keys(src, carry):
+        @pl.when(z > 0)
+        def _():
+            for copy in relay_key(src):
+                copy.wait_recv()
+
+        return carry
+
+    lax.fori_loop(0, width, take_keys, 0)
 
     scale = HEAD**-0.5 * math.log2(math.e)
     tri = lax.broadcasted_iota(jnp.int32, (TOK, TOK), 0) >= lax.broadcasted_iota(
@@ -550,7 +558,26 @@
             total = jnp.sum(total, axis=1, keepdims=True)
             linv[b, h] = jnp.broadcast_to(1.0 / total, (TOK, TOK))
 
+    own_v.wait()
+
+    def relay_value(src):
+        return remote(v_all.at[width + src], v_all.at[src], f_ss.at[src], f_rs.at[src], next_plane)
+
+    def relay_factor(src):
+        return remote(r_all.at[width + src], r_all.at[src], gf_ss.at[src], gf_rs.at[src], next_plane)
+
     def weigh(i, carry):
+        src = ring(w, -i, width)
+        slot = width + src
+
+        @pl.when(i != 0)
+        def _():
+            remote(v_all.at[slot], v_all.at[slot], v_ss.at[0], v_rs.at[src], next_seq).wait_recv()
+
+        @pl.when(z < planes - 1)
+        def _():
+            relay_value(src).start()
+
         weights(i)
         return carry
 
@@ -569,16 +596,17 @@
             col = slice(part * 128, (part + 1) * 128)
             v_s[slot, :, col] = (v_all[slot, :, col].astype(F32) * factor).astype(BF16)
 
-    own_v.wait()
-
     def take_own(i, carry):
         src = ring(w, -i, width)
         slot = width + src
 
         @pl.when(i != 0)
         def _():
-            remote(v_all.at[slot], v_all.at[slot], v_ss.at[0], v_rs.at[src], next_seq).wait_recv()
-            remote(r_all.at[slot], r_all.at[slot], g_ss.at[0], g_rs.at[slot], next_seq).wait_recv()
+            remote(r_all.at[slot], r_all.at[slot], g_ss.at[0], g_rs.at[src], next_seq).wait_recv()
+
+        @pl.when(z < planes - 1)
+        def _():
+            relay_factor(src).start()
 
         scale_values(slot)
         return carry
@@ -595,8 +623,11 @@
             )
 
     for b in range(width - 1, -1, -1):
-        remote(v_all.at[b], v_all.at[b], v_ss.at[0], f_rs.at[b], next_seq).wait_recv()
-        remote(r_all.at[b], r_all.at[b], g_ss.at[0], g_rs.at[b], next_seq).wait_recv()
+        @pl.when(z > 0)
+        def _():
+            relay_value(b).wait_recv()
+            relay_factor(b).wait_recv()
+
         scale_values(b)
         squares = None
         for h in range(heads):
@@ -678,6 +709,10 @@
         copy.wait_send()
 
     def drain(j, carry):
+        @pl.when(z < planes - 1)
+        def _():
+            for copy in (*relay_key(j), relay_value(j), relay_factor(j)):
+                copy.wait_send()
         @pl.when(j != w)
         def _():
             remote(
@@ -777,10 +812,16 @@
             dma((width,)),
             dma((width,)),
             dma((width,)),
-            dma((width + 2,)),
-            dma((width + 2,)),
-            dma((2 * width,)),
-            dma((2 * width,)),
+            dma((width,)),
+            dma((width,)),
+            dma((width,)),
+            dma((width,)),
+            dma((width,)),
+            dma((width,)),
+            dma((width,)),
+            dma((width,)),
+            dma((width,)),
+            dma((width,)),
             dma((width,)),
             dma((width,)),
             dma((3, mps)),

time: 70.8 us -> 69 us (0.975)
  the two profiles are of different devices: /device:TPU:1 before, /device:TPU:33 now
where the time goes in v3:
time: 69 us; the launch traced here: 68.9 us
  Pallas kernels  65.5 us (95%)
  local copies, waits for them, and re-layouts  2.74 us (4%)
    pallas_call x1, Pallas kernels, local(): pl.pallas_call(functools.partial(kernel, planes, width, mps, d_model), ou...  65.5 us
    unnamed x4, local copies, waits for them, and re-layouts  2.74 us

profile of v3, /device:TPU:33, one launch (start us, length us, event | category | flops | bytes accessed | tf_op | source)
XLA Modules:
  0.0 68.9 jit_solution(13935808546951595801)
XLA Ops:
  0.6 65.5 %shard_map.167 = (bf16[128,2048]{1,0:T(8,128)(2,1)}, bf16[128,2048]{1,0:T(8,128)(2,1)}) custom-call(bf16[128,2048]{1,0:T(8,128)(2,1)} %se_q_h.1, bf16[128,2048]{1,0:T(8,128)(2,1)} %se_k_h.1, bf16[128,2048]{1,0:T(8,128)(2,1)} %se_v_h.1, bf16[128,2048]{1,0:T(8,128)(2,1)} %mr_q_h.1, bf16[128,2048]{1,0:T(8,128)(2,1)} %mr_k_h.1, bf16[128,2048]{1,0:T(8,128)(2,1)} %att_q.1, ...), custom_call_target="tpu_custom_call" | custom-call | tf_op jit(solution)/shard_map/pallas_call | solution.py:738
  66.1 0.0 copy-start
  66.1 1.9 %copy.20 = bf16[128,2048]{1,0:T(8,128)(2,1)} copy(bf16[128,2048]{1,0:T(8,128)(2,1)} %get-tuple-element.4) | data formatting | bytes 1048576
  68.1 0.0 copy-done
  68.1 0.8 %copy.21 = bf16[128,2048]{1,0:T(8,128)(2,1)} copy(bf16[128,2048]{1,0:T(8,128)(2,1)S(1)} %copy-done) | data formatting | bytes 1048576
Async XLA Ops:
  66.1 2.0 %copy-start = (bf16[128,2048]{1,0:T(8,128)(2,1)S(1)}, bf16[128,2048]{1,0:T(8,128)(2,1)}, u32[]{:S(2)}) copy-start(bf16[128,2048]{1,0:T(8,128)(2,1)} %get-tuple-element.5) | copy-start | bytes 1572868

commit v4 on v3

--- a/solution.py
+++ b/solution.py
@@ -419,10 +419,11 @@
         return carry
 
     def relay_key(src):
-        return (
-            remote(k_all.at[width + src], k_all.at[src], kf_ss.at[src], kf_rs.at[src], next_plane),
-            remote(id_all.at[width + src], id_all.at[src], if_ss.at[src], if_rs.at[src], next_plane),
-        )
+        return remote(k_all.at[width + src], k_all.at[src], kf_ss.at[src], kf_rs.at[src], next_plane)
+
+    id_up = remote(
+        id_all.at[pl.ds(width, width)], id_all.at[pl.ds(0, width)], if_ss.at[0], if_rs.at[0], next_plane
+    )
 
     def medium_and_relay(g, carry):
         medium_part(g, carry)
@@ -437,8 +438,7 @@
 
         @pl.when(z < planes - 1)
         def _():
-            for copy in relay_key(src):
-                copy.start()
+            relay_key(src).start()
 
         return carry
 
@@ -446,6 +446,7 @@
     lax.fori_loop(0, relay_from, medium_part, 0)
     own_k.wait()
     lax.fori_loop(relay_from, groups, medium_and_relay, 0)
+    pl.when(z < planes - 1)(id_up.start)
 
     loaded(mr_q, mr_gain, att_gain, back)
     r_next.wait_recv()
@@ -518,12 +519,12 @@
     def take_keys(src, carry):
         @pl.when(z > 0)
         def _():
-            for copy in relay_key(src):
-                copy.wait_recv()
+            relay_key(src).wait_recv()
 
         return carry
 
     lax.fori_loop(0, width, take_keys, 0)
+    pl.when(z > 0)(id_up.wait_recv)
 
     scale = HEAD**-0.5 * math.log2(math.e)
     tri = lax.broadcasted_iota(jnp.int32, (TOK, TOK), 0) >= lax.broadcasted_iota(
@@ -563,8 +564,9 @@
     def relay_value(src):
         return remote(v_all.at[width + src], v_all.at[src], f_ss.at[src], f_rs.at[src], next_plane)
 
-    def relay_factor(src):
-        return remote(r_all.at[width + src], r_all.at[src], gf_ss.at[src], gf_rs.at[src], next_plane)
+    r_up = remote(
+        r_all.at[pl.ds(width, width)], r_all.at[pl.ds(0, width)], gf_ss.at[0], gf_rs.at[0], next_plane
+    )
 
     def weigh(i, carry):
         src = ring(w, -i, width)
@@ -596,19 +598,17 @@
             col = slice(part * 128, (part + 1) * 128)
             v_s[slot, :, col] = (v_all[slot, :, col].astype(F32) * factor).astype(BF16)
 
-    def take_own(i, carry):
+    def take_factor(i, carry):
         src = ring(w, -i, width)
         slot = width + src
-
-        @pl.when(i != 0)
-        def _():
-            remote(r_all.at[slot], r_all.at[slot], g_ss.at[0], g_rs.at[src], next_seq).wait_recv()
-
-        @pl.when(z < planes - 1)
-        def _():
-            relay_factor(src).start()
-
-        scale_values(slot)
+        remote(r_all.at[slot], r_all.at[slot], g_ss.at[0], g_rs.at[src], next_seq).wait_recv()
+        return carry
+
+    lax.fori_loop(1, width, take_factor, 0)
+    pl.when(z < planes - 1)(r_up.start)
+
+    def take_own(i, carry):
+        scale_values(width + i)
         return carry
 
     lax.fori_loop(0, width, take_own, 0)
@@ -626,7 +626,8 @@
         @pl.when(z > 0)
         def _():
             relay_value(b).wait_recv()
-            relay_factor(b).wait_recv()
+            if b == width - 1:
+                r_up.wait_recv()
 
         scale_values(b)
         squares = None
@@ -711,8 +712,8 @@
     def drain(j, carry):
         @pl.when(z < planes - 1)
         def _():
-            for copy in (*relay_key(j), relay_value(j), relay_factor(j)):
-                copy.wait_send()
+            relay_key(j).wait_send()
+            relay_value(j).wait_send()
         @pl.when(j != w)
         def _():
             remote(
@@ -722,6 +723,11 @@
         return carry
 
     lax.fori_loop(0, width, drain, 0)
+
+    @pl.when(z < planes - 1)
+    def _():
+        id_up.wait_send()
+        r_up.wait_send()
 
 
 def local(planes, width, mps, d_model, *args):
@@ -818,10 +824,10 @@
             dma((width,)),
             dma((width,)),
             dma((width,)),
-            dma((width,)),
-            dma((width,)),
-            dma((width,)),
-            dma((width,)),
+            dma((1,)),
+            dma((1,)),
+            dma((1,)),
+            dma((1,)),
             dma((width,)),
             dma((width,)),
             dma((3, mps)),

time: 69 us -> 68.8 us (level)
  no operation moved by 1% of the time
where the time goes in v4:
time: 68.8 us; the launch traced here: 68.7 us
  Pallas kernels  65.3 us (95%)
  local copies, waits for them, and re-layouts  2.74 us (4%)
    pallas_call x1, Pallas kernels, local(): pl.pallas_call(functools.partial(kernel, planes, width, mps, d_model), ou...  65.3 us
    unnamed x4, local copies, waits for them, and re-layouts  2.74 us

profile of v4, /device:TPU:33, one launch (start us, length us, event | category | flops | bytes accessed | tf_op | source)
XLA Modules:
  0.0 68.7 jit_solution(13507731383366217202)
XLA Ops:
  0.6 65.3 %shard_map.167 = (bf16[128,2048]{1,0:T(8,128)(2,1)}, bf16[128,2048]{1,0:T(8,128)(2,1)}) custom-call(bf16[128,2048]{1,0:T(8,128)(2,1)} %se_q_h.1, bf16[128,2048]{1,0:T(8,128)(2,1)} %se_k_h.1, bf16[128,2048]{1,0:T(8,128)(2,1)} %se_v_h.1, bf16[128,2048]{1,0:T(8,128)(2,1)} %mr_q_h.1, bf16[128,2048]{1,0:T(8,128)(2,1)} %mr_k_h.1, bf16[128,2048]{1,0:T(8,128)(2,1)} %att_q.1, ...), custom_call_target="tpu_custom_call" | custom-call | tf_op jit(solution)/shard_map/pallas_call | solution.py:744
  65.9 0.0 copy-start
  65.9 1.9 %copy.20 = bf16[128,2048]{1,0:T(8,128)(2,1)} copy(bf16[128,2048]{1,0:T(8,128)(2,1)} %get-tuple-element.4) | data formatting | bytes 1048576
  67.9 0.0 copy-done
  67.9 0.8 %copy.21 = bf16[128,2048]{1,0:T(8,128)(2,1)} copy(bf16[128,2048]{1,0:T(8,128)(2,1)S(1)} %copy-done) | data formatting | bytes 1048576
Async XLA Ops:
  65.9 2.0 %copy-start = (bf16[128,2048]{1,0:T(8,128)(2,1)S(1)}, bf16[128,2048]{1,0:T(8,128)(2,1)}, u32[]{:S(2)}) copy-start(bf16[128,2048]{1,0:T(8,128)(2,1)} %get-tuple-element.5) | copy-start | bytes 1572868
